TPU v7x, 512 devices: a whole 4x4x16 slice. The times are simulated.
512 devices in a mesh: dp: 32 (over y, z_lo, core), tensor: 16 (over x, z_hi).
Axes of the slice: x: 4, y: 4, z: 16 (z_hi: 4, z_lo: 4; z = z_hi * 4 + z_lo), core: 2. Of those that a mesh axis runs over, the one named last changes fastest.
Arguments:
- tokens: bfloat16 [131072, 4096], P(('dp', 'tensor')), may hold values from -6 to 6
- cotangent: bfloat16 [131072, 4096], P(('dp', 'tensor')), may hold values from -0.29882812 to 0.29882812
- routes: int32 [131072, 8], P(('dp', 'tensor')), may hold values from 0 to 127, as said below
- combine: float32 [131072, 8], P(('dp', 'tensor')), may hold values from 0.05 to 1
- gate_up_codes: int32 [2, 4096, 4096], P(None, 'tensor', 'dp'), may hold values from 0 to 15
- gate_up_scales: float32 [2, 4096, 128], P(None, 'tensor', 'dp'), may hold values from 0.003 to 0.01
- down_codes: int32 [4096, 4096], P('tensor', 'dp'), may hold values from 0 to 15
- down_scales: float32 [128, 4096], P('tensor', 'dp'), may hold values from 0.004 to 0.016
Outputs:
- gate_up_grad: float32 [2, 4096, 4096], P(None, 'tensor', 'dp')
- gate_up_scale_grad: float32 [2, 4096, 128], P(None, 'tensor', 'dp')
Inputs may be any that keep to these rules, and one draw needn't show every extreme that they name: `routes`: each row names 8 different experts. For each expert e < 4, in the rows of one device at most 20 name e, and in every draw the rows of some device have exactly 20 that name e.
All inputs are finite; a program needn't handle non-finite values.
Results may differ from a plain program's by a relative error of at most 0.029.
Values may be sent and summed in bfloat16 or wider, within the bound.
A program may use at most 64 MiB of HBM per device.

v0:
```python
import jax
import jax.numpy as jnp
from jax import lax
from jax.sharding import PartitionSpec as P

BLOCK = 32
GROUP = 4
CAP = 20


lsq_factor = 192.0 ** (-0.5)


def decode_values(code_array):
    modulus = (code_array % 8).astype(jnp.float32)
    levels = jnp.where(
        modulus < 4.0,
        0.5 * modulus,
        jnp.where(modulus < 6.0, modulus - 2.0, jnp.where(modulus < 7.0, 4.0, 6.0)),
    )
    sign_part = 1.0 - 2.0 * (code_array // 8).astype(jnp.float32)
    return sign_part * levels


def body(
    tokens, cotangent, routes, combine, gate_up_codes, gate_up_scales, down_codes, down_scales
):
    expert_count = lax.axis_size("tensor") // GROUP
    expert_ids = jnp.arange(expert_count, dtype=jnp.int32)
    chosen = routes[:, :, None] == expert_ids[None, None, :]
    is_routed = jnp.any(chosen, axis=1)
    weight = jnp.sum(
        jnp.where(chosen, combine[:, :, None], jnp.zeros_like(combine)[:, :, None]), axis=1
    )
    slot_index = jnp.cumsum(is_routed.astype(jnp.int32), axis=0) - 1
    one_hot = (
        slot_index.T[:, None, :] == jnp.arange(CAP, dtype=jnp.int32)[None, :, None]
    ) & is_routed.T[:, None, :]
    selector = one_hot.astype(jnp.bfloat16)
    picked_tokens = jnp.einsum(
        "ect,td->ecd", selector, tokens, preferred_element_type=jnp.float32
    ).astype(jnp.bfloat16)
    picked_cot = jnp.einsum("ect,td->ecd", selector, cotangent, preferred_element_type=jnp.float32)
    picked_weight = jnp.sum(one_hot.astype(jnp.float32) * weight.T[:, None, :], axis=2)
    picked_scaled = (picked_weight[:, :, None] * picked_cot).astype(jnp.bfloat16)
    send_tokens = jnp.repeat(picked_tokens, GROUP, axis=0)
    send_scaled = jnp.repeat(picked_scaled, GROUP, axis=0)
    token_block, scaled_block = (
        lax.all_to_all(send_tokens, "tensor", split_axis=0, concat_axis=0, tiled=True),
        lax.all_to_all(send_scaled, "tensor", split_axis=0, concat_axis=0, tiled=True),
    )
    width_full = tokens.shape[1]
    token_rows = token_block.reshape(-1, width_full)
    scaled_rows = scaled_block.reshape(-1, width_full)
    gate_up_values = decode_values(gate_up_codes)
    down_values = decode_values(down_codes)
    hidden_local = gate_up_codes.shape[1]
    width_local = gate_up_codes.shape[2]
    gate_up_weight = (
        (
            gate_up_values.reshape(2, hidden_local, width_local // BLOCK, BLOCK)
            * gate_up_scales[..., None]
        )
        .reshape(2, hidden_local, width_local)
        .astype(jnp.bfloat16)
    )
    down_weight = (
        (down_values.reshape(hidden_local // BLOCK, BLOCK, width_local) * down_scales[:, None, :])
        .reshape(hidden_local, width_local)
        .astype(jnp.bfloat16)
    )
    stacked = jnp.concatenate([gate_up_weight, down_weight[None]], axis=0)
    gathered = lax.all_gather(stacked, "dp", axis=2, tiled=True)
    projected = jnp.einsum(
        "rd,gfd->grf", token_rows, gathered[:2], preferred_element_type=jnp.float32
    )
    back_hidden = jnp.einsum(
        "rd,fd->rf", scaled_rows, gathered[2], preferred_element_type=jnp.float32
    )
    pre_gate = projected[0]
    pre_up = projected[1]
    sigmoid_gate = jax.nn.sigmoid(pre_gate)
    silu_gate = pre_gate * sigmoid_gate
    grad_gate = (
        back_hidden * pre_up * sigmoid_gate * (1.0 + pre_gate * (1.0 - sigmoid_gate))
    ).astype(jnp.bfloat16)
    grad_up = (back_hidden * silu_gate).astype(jnp.bfloat16)
    grad_pair = jnp.stack([grad_gate, grad_up])
    partial_sum = jnp.einsum(
        "grf,rd->gfd", grad_pair, token_rows, preferred_element_type=jnp.float32
    )
    summed = lax.psum_scatter(
        partial_sum.astype(jnp.bfloat16), "dp", scatter_dimension=2, tiled=True
    ).astype(jnp.float32)
    gate_up_grad = jnp.where(gate_up_codes % 8 != 7, summed, jnp.zeros_like(summed))
    gate_up_scale_grad = lsq_factor * jnp.sum(
        (summed * gate_up_values).reshape(2, hidden_local, width_local // BLOCK, BLOCK), axis=-1
    )
    return (gate_up_grad, gate_up_scale_grad)


def solution(mesh):
    return jax.shard_map(
        body,
        mesh=mesh,
        in_specs=(
            P(("dp", "tensor"), None),
            P(("dp", "tensor"), None),
            P(("dp", "tensor"), None),
            P(("dp", "tensor"), None),
            P(None, "tensor", "dp"),
            P(None, "tensor", "dp"),
            P("tensor", "dp"),
            P("tensor", "dp"),
        ),
        out_specs=(P(None, "tensor", "dp"), P(None, "tensor", "dp")),
        check_vma=False,
    )
```

profile of v0, /device:TPU:1, one launch (start us, length us, event | category | flops | bytes accessed | tf_op | source)
XLA Modules:
  0.0 537.8 jit_solution(4115585790245474724)
XLA Ops:
  7.2 0.9 fusion.35
  8.1 1.2 reduce-window.6
  9.4 0.1 copy.27
  9.5 0.1 copy.28
  9.6 0.1 add_bitcast_fusion
  9.7 0.7 select_reduce_fusion.1
  10.4 0.1 select_reduce_fusion
  10.5 0.5 fusion
  11.0 2.0 broadcast_in_dim.48
  13.0 18.4 %all-to-all-start = ((bf16[16,20,4096]{2,1,0:T(8,128)(2,1)}), bf16[16,20,4096]{2,1,0:T(8,128)(2,1)}, u32[]{:S(2)}, u32[]{:S(2)}) async-start(bf16[16,20,4096]{2,1,0:T(8,128)(2,1)} %bitcast.66), calls=%async_computation | async-start | bytes 6291456 | tf_op jit(solution)/shard_map/all_to_all | solution.py:50
  31.5 0.1 copy.29
  31.7 0.2 fusion.24
  31.9 0.4 multiply_convert_fusion.1
  32.2 0.7 pad_maximum_fusion
  32.9 2.1 convolution_convert_fusion.1
  35.0 133.1 %all-to-all-done = bf16[16,20,4096]{2,1,0:T(8,128)(2,1)} async-done(((bf16[16,20,4096]{2,1,0:T(8,128)(2,1)}), bf16[16,20,4096]{2,1,0:T(8,128)(2,1)}, u32[]{:S(2)}, u32[]{:S(2)}) %all-to-all-start) | async-done | bytes 2621472 | tf_op jit(solution)/shard_map/all_to_all | solution.py:50
  168.1 2.0 broadcast_in_dim.50
  170.1 10.1 %all-to-all-start.1 = ((bf16[16,20,4096]{2,1,0:T(8,128)(2,1)}), bf16[16,20,4096]{2,1,0:T(8,128)(2,1)}, u32[]{:S(2)}, u32[]{:S(2)}) async-start(bf16[16,20,4096]{2,1,0:T(8,128)(2,1)} %bitcast.67), calls=%async_computation.1 | async-start | bytes 6291456 | tf_op jit(solution)/shard_map/all_to_all | solution.py:49
  180.2 4.3 reshape.49
  184.5 159.6 %all-to-all-done.1 = bf16[16,20,4096]{2,1,0:T(8,128)(2,1)} async-done(((bf16[16,20,4096]{2,1,0:T(8,128)(2,1)}), bf16[16,20,4096]{2,1,0:T(8,128)(2,1)}, u32[]{:S(2)}, u32[]{:S(2)}) %all-to-all-start.1) | async-done | bytes 2621472 | tf_op jit(solution)/shard_map/all_to_all | solution.py:49
  344.1 4.3 reshape.56
  348.5 4.7 convolution_bitcast_fusion
  353.2 2.7 fusion.18
  355.9 4.4 convolution_convert_fusion
  360.2 11.1 %copy.31 = bf16[2,256,4096]{1,0,2:T(2,128)(2,1)} copy(bf16[2,256,4096]{2,1,0:T(8,128)(2,1)} %convolution_convert_fusion) | data formatting | bytes 8388608
  371.3 4.9 copy.34
  376.3 151.8 %reduce-scatter.4.cloned.1.call-done = bf16[128,512]{1,0:T(8,128)(2,1)} async-done(((bf16[4096,512]{1,0:T(8,128)(2,1)}), bf16[128,512]{1,0:T(8,128)(2,1)}) %reduce-scatter.4.cloned.1.call-update) | async-done | bytes 131088
  528.0 0.9 reshape.59
  529.0 0.1 copy.32
  529.1 1.1 convert_multiply_fusion
  530.2 0.1 copy.30
  530.4 0.6 broadcast_multiply_fusion
  (27 shorter events, 0.4 us)
Async XLA Ops:
  7.2 3.4 copy-start
  13.0 18.5 %copy-start.5 = (f32[2,256,4]{1,2,0:T(4,128)S(1)}, f32[2,256,4]{1,2,0:T(4,128)}, u32[]{:S(2)}) copy-start(f32[2,256,4]{1,2,0:T(4,128)} %param.13) | copy-start | bytes 24580
  13.0 18.6 %copy-start.4 = (s32[256,128]{1,0:T(8,128)S(1)}, s32[256,128]{1,0:T(8,128)}, u32[]{:S(2)}) copy-start(s32[256,128]{1,0:T(8,128)} %param.14) | copy-start | bytes 393220
  13.0 18.6 %copy-start.6 = (f32[8,128]{1,0:T(8,128)S(1)}, f32[8,128]{1,0:T(8,128)}, u32[]{:S(2)}) copy-start(f32[8,128]{1,0:T(8,128)} %param.15) | copy-start | bytes 12292
  13.0 18.8 %copy-start.3 = (s32[2,256,128]{2,1,0:T(8,128)S(1)}, s32[2,256,128]{2,1,0:T(8,128)}, u32[]{:S(2)}) copy-start(s32[2,256,128]{2,1,0:T(8,128)} %param.12) | copy-start | bytes 786436
  13.0 155.0 %all-to-all-start = ((bf16[16,20,4096]{2,1,0:T(8,128)(2,1)}), bf16[16,20,4096]{2,1,0:T(8,128)(2,1)}, u32[]{:S(2)}, u32[]{:S(2)}) async-start(bf16[16,20,4096]{2,1,0:T(8,128)(2,1)} %bitcast.66), calls=%async_computation | async-start | bytes 6291456 | tf_op jit(solution)/shard_map/all_to_all | solution.py:50
  31.4 317.1 %all-gather.2.cloned.1.call-start = ((), (), s32[]{:S(2)}) async-start(), calls=%async_computation.3 | async-start | bytes 6488064 | tf_op jit(solution)/shard_map/all_gather | solution.py:73
  170.1 174.0 %all-to-all-start.1 = ((bf16[16,20,4096]{2,1,0:T(8,128)(2,1)}), bf16[16,20,4096]{2,1,0:T(8,128)(2,1)}, u32[]{:S(2)}, u32[]{:S(2)}) async-start(bf16[16,20,4096]{2,1,0:T(8,128)(2,1)} %bitcast.67), calls=%async_computation.1 | async-start | bytes 6291456 | tf_op jit(solution)/shard_map/all_to_all | solution.py:49
  180.2 347.9 %reduce-scatter.4.cloned.1.call-start = ((), (), s32[]{:S(2)}) async-start(), calls=%async_computation.4 | async-start | bytes 4325376
  348.5 4.7 copy-start.1
  353.2 2.7 copy-start.2
Sparse Core Ops, SparseCore 0:
  34.9 306.7 all-gather.1
  376.4 151.6 reduce-scatter.3
where the time goes:
time: 543 us; the launch traced here: 538 us
  waiting for transfers between devices  444 us (82%)
  local copies, waits for them, and re-layouts  30.4 us (6%)
  starting transfers between devices  28.5 us (5%)
  matrix products  14.2 us (3%)
  between operations  14.2 us (3%)
  other arithmetic  6 us (1%)
    all_to_all x1, waiting for transfers between devices, body(): lax.all_to_all(send_tokens, 'tensor', split_axis=0, concat_axis=0, tiled=...  160 us
    unnamed x3, waiting for transfers between devices  152 us
    all_to_all x1, waiting for transfers between devices, body(): lax.all_to_all(send_scaled, 'tensor', split_axis=0, concat_axis=0, tiled=...  133 us
    all_to_all x1, starting transfers between devices, body(): lax.all_to_all(send_scaled, 'tensor', split_axis=0, concat_axis=0, tiled=...  18.4 us
    unnamed x19, local copies, waits for them, and re-layouts  17.1 us
  transfers between devices with their start and end apart: 4, of which 3 were waited for; matrix products, arithmetic and copies ran while one was open for 3% of the time, Pallas kernels for 0%

commit v1 on v0

--- a/solution.py
+++ b/solution.py
@@ -1,11 +1,13 @@
 import jax
 import jax.numpy as jnp
 from jax import lax
+from jax.sharding import Mesh
 from jax.sharding import PartitionSpec as P
 
 BLOCK = 32
-GROUP = 4
 CAP = 20
+SIDE = 4
+SWAP = [(p * SIDE + q, q * SIDE + p) for p in range(SIDE) for q in range(SIDE)]
 
 
 lsq_factor = 192.0 ** (-0.5)
@@ -25,7 +27,7 @@
 def body(
     tokens, cotangent, routes, combine, gate_up_codes, gate_up_scales, down_codes, down_scales
 ):
-    expert_count = lax.axis_size("tensor") // GROUP
+    expert_count = lax.axis_size("x")
     expert_ids = jnp.arange(expert_count, dtype=jnp.int32)
     chosen = routes[:, :, None] == expert_ids[None, None, :]
     is_routed = jnp.any(chosen, axis=1)
@@ -43,12 +45,10 @@
     picked_cot = jnp.einsum("ect,td->ecd", selector, cotangent, preferred_element_type=jnp.float32)
     picked_weight = jnp.sum(one_hot.astype(jnp.float32) * weight.T[:, None, :], axis=2)
     picked_scaled = (picked_weight[:, :, None] * picked_cot).astype(jnp.bfloat16)
-    send_tokens = jnp.repeat(picked_tokens, GROUP, axis=0)
-    send_scaled = jnp.repeat(picked_scaled, GROUP, axis=0)
-    token_block, scaled_block = (
-        lax.all_to_all(send_tokens, "tensor", split_axis=0, concat_axis=0, tiled=True),
-        lax.all_to_all(send_scaled, "tensor", split_axis=0, concat_axis=0, tiled=True),
-    )
+    picked = jnp.stack([picked_tokens, picked_scaled], axis=1)
+    own_expert = lax.all_to_all(picked, "x", split_axis=0, concat_axis=0, tiled=True)
+    pooled = lax.all_gather(own_expert, ("y", "c"), axis=0, tiled=True)
+    token_block, scaled_block = pooled[:, 0], pooled[:, 1]
     width_full = tokens.shape[1]
     token_rows = token_block.reshape(-1, width_full)
     scaled_rows = scaled_block.reshape(-1, width_full)
@@ -70,7 +70,9 @@
         .astype(jnp.bfloat16)
     )
     stacked = jnp.concatenate([gate_up_weight, down_weight[None]], axis=0)
-    gathered = lax.all_gather(stacked, "dp", axis=2, tiled=True)
+    halves = lax.all_to_all(stacked, "c", split_axis=1, concat_axis=2, tiled=True)
+    swapped = lax.ppermute(halves, ("y", "zh"), SWAP)
+    gathered = lax.all_gather(swapped, ("zh", "zl"), axis=2, tiled=True)
     projected = jnp.einsum(
         "rd,gfd->grf", token_rows, gathered[:2], preferred_element_type=jnp.float32
     )
@@ -89,9 +91,11 @@
     partial_sum = jnp.einsum(
         "grf,rd->gfd", grad_pair, token_rows, preferred_element_type=jnp.float32
     )
-    summed = lax.psum_scatter(
-        partial_sum.astype(jnp.bfloat16), "dp", scatter_dimension=2, tiled=True
-    ).astype(jnp.float32)
+    scattered = lax.psum_scatter(
+        partial_sum.astype(jnp.bfloat16), ("zh", "zl"), scatter_dimension=2, tiled=True
+    )
+    back = lax.ppermute(scattered, ("y", "zh"), SWAP)
+    summed = lax.all_to_all(back, "c", split_axis=2, concat_axis=1, tiled=True).astype(jnp.float32)
     gate_up_grad = jnp.where(gate_up_codes % 8 != 7, summed, jnp.zeros_like(summed))
     gate_up_scale_grad = lsq_factor * jnp.sum(
         (summed * gate_up_values).reshape(2, hidden_local, width_local // BLOCK, BLOCK), axis=-1
@@ -100,19 +104,24 @@
 
 
 def solution(mesh):
+    fine = Mesh(
+        mesh.devices.reshape(SIDE, SIDE, 2, SIDE, SIDE), ("y", "zl", "c", "x", "zh")
+    )
+    dp, tensor = ("y", "zl", "c"), ("x", "zh")
+    rows = P(dp + tensor, None)
     return jax.shard_map(
         body,
-        mesh=mesh,
+        mesh=fine,
         in_specs=(
-            P(("dp", "tensor"), None),
-            P(("dp", "tensor"), None),
-            P(("dp", "tensor"), None),
-            P(("dp", "tensor"), None),
-            P(None, "tensor", "dp"),
-            P(None, "tensor", "dp"),
-            P("tensor", "dp"),
-            P("tensor", "dp"),
+            rows,
+            rows,
+            rows,
+            rows,
+            P(None, tensor, dp),
+            P(None, tensor, dp),
+            P(tensor, dp),
+            P(tensor, dp),
         ),
-        out_specs=(P(None, "tensor", "dp"), P(None, "tensor", "dp")),
+        out_specs=(P(None, tensor, dp), P(None, tensor, dp)),
         check_vma=False,
     )

time: 543 us -> 312 us (0.57)
  the two profiles are of different devices: /device:TPU:1 before, /device:TPU:17 now
where the time goes in v1:
time: 312 us
  waiting for transfers between devices  140 us (45%)
  local copies, waits for them, and re-layouts  73.3 us (23%)
  blocking collectives  42 us (13%)
  starting transfers between devices  24.8 us (8%)
  between operations  14 us (4%)
  matrix products  12.9 us (4%)
  other arithmetic  5 us (2%)
    reduce_scatter x1, waiting for transfers between devices, body(): lax.psum_scatter(partial_sum.astype(jnp.bfloat16), ('zh', 'zl'), scatter_...  67.5 us
    slice x1, local copies, waits for them, and re-layouts, body(): token_block, scaled_block = (pooled[:, 0], pooled[:, 1])  53 us
    all_gather x1, waiting for transfers between devices, body(): pooled = lax.all_gather(own_expert, ('y', 'c'), axis=0, tiled=True)  43.9 us
    all_to_all x1, blocking collectives, body(): lax.all_to_all(picked, 'x', split_axis=0, concat_axis=0, tiled=True)  21 us
    all_to_all x1, blocking collectives, body(): lax.all_to_all(back, 'c', split_axis=2, concat_axis=1, tiled=True)  15.5 us
    ppermute x1, starting transfers between devices, body(): swapped = lax.ppermute(halves, ('y', 'zh'), SWAP)  15.2 us
    all_gather x1, waiting for transfers between devices, body(): gathered = lax.all_gather(swapped, ('zh', 'zl'), axis=2, tiled=True)  14.8 us
    ppermute x1, starting transfers between devices, body(): back = lax.ppermute(scattered, ('y', 'zh'), SWAP)  9.27 us
  transfers between devices with their start and end apart: 5, of which 5 were waited for; matrix products, arithmetic and copies ran while one was open for 22% of the time, Pallas kernels for 0%

profile of v1, /device:TPU:17, one launch (start us, length us, event | category | flops | bytes accessed | tf_op | source)
XLA Modules:
  0.0 311.6 jit_solution(10919302154041552350)
XLA Ops:
  7.2 0.9 fusion.39
  8.1 1.2 reduce-window.6
  9.7 0.9 select_reduce_fusion.1
  10.7 0.5 fusion.2
  11.3 0.5 fusion.1
  11.7 0.2 pad_maximum_fusion
  12.0 1.4 copy.102
  13.4 21.0 %all_to_all.32 = bf16[4,2,20,4096]{3,1,2,0:T(2,128)(2,1)} all-to-all(bf16[4,2,20,4096]{3,1,2,0:T(2,128)(2,1)S(1)} %copy.102), channel_id=1, replica_groups=mesh['y'=4,'zl'=4,'c'=2,'x'=4,'zh'=4] {'x'}, dimensions={0} | all-to-all | bytes 2621440 | tf_op jit(solution)/shard_map/all_to_all | solution.py:49
  34.9 0.3 fusion.17
  35.2 0.2 fusion.34
  35.6 5.5 %all_to_all.33 = bf16[3,256,128]{2,0,1:T(4,128)(2,1)S(1)} all-to-all(bf16[3,256,128]{2,0,1:T(4,128)(2,1)S(1)} %copy.109), channel_id=1, replica_groups=mesh['y'=4,'zl'=4,'c'=2,'x'=4,'zh'=4] {'c'}, dimensions={1} | all-to-all | bytes 393216 | tf_op jit(solution)/shard_map/all_to_all | solution.py:73
  41.1 0.2 copy.125
  41.5 15.2 %collective-permute-start = (bf16[3,128,256]{2,1,0:T(8,128)(2,1)S(1)}, bf16[3,128,256]{2,1,0:T(8,128)(2,1)S(1)}, u32[]{:S(2)}, u32[]{:S(2)}) collective-permute-start(bf16[3,128,256]{2,1,0:T(8,128)(2,1)S(1)} %all_to_all.27), channel_id=1, source_target_pairs={{0,0},{1,128},{2,256},{3,384},{128,1},{129,129},{130,257},{131,385... | collective-permute-start | bytes 589832 | tf_op jit(solution)/shard_map/ppermute | solution.py:74
  56.7 5.1 %collective-permute-done = bf16[3,128,256]{2,1,0:T(8,128)(2,1)S(1)} collective-permute-done((bf16[3,128,256]{2,1,0:T(8,128)(2,1)S(1)}, bf16[3,128,256]{2,1,0:T(8,128)(2,1)S(1)}, u32[]{:S(2)}, u32[]{:S(2)}) %collective-permute-start) | collective-permute-done | bytes 196640 | tf_op jit(solution)/shard_map/ppermute | solution.py:74
  61.8 0.7 copy-done.3
  62.5 0.2 reduce-scatter.2.cloned.1.call-start
  62.8 43.9 %all-gather.3.cloned.1.call-done = bf16[32,2,20,4096]{3,1,2,0:T(2,128)(2,1)} async-done(((bf16[4,2,20,4096]{3,1,2,0:T(2,128)(2,1)}), bf16[32,2,20,4096]{3,1,2,0:T(2,128)(2,1)}) %all-gather.3.cloned.1.call-update) | async-done | bytes 10485776 | tf_op jit(solution)/shard_map/all_gather | solution.py:50
  106.7 53.0 %slice_reduce_fusion.1 = (bf16[32,20,4096]{2,1,0:T(8,128)(2,1)}, bf16[32,20,4096]{2,1,0:T(8,128)(2,1)}) fusion(bf16[32,2,20,4096]{3,1,2,0:T(2,128)(2,1)} %all-gather.3.cloned.1.call-done), kind=kLoop, calls=%fused_computation.1 | loop fusion | bytes 20971520 | tf_op jit(solution)/shard_map/slice | solution.py:51
  159.7 7.8 %reshape.46 = bf16[640,4096,1]{1,0,2:T(8,128)(2,1)} reshape(bf16[32,20,4096]{2,1,0:T(8,128)(2,1)} %get-tuple-element.13) | data formatting | bytes 10485760 | tf_op jit(solution)/shard_map/reshape;squeeze | solution.py:53
  167.6 7.8 %reshape_squeeze.6 = bf16[640,4096]{1,0:T(8,128)(2,1)} reshape(bf16[32,20,4096]{2,1,0:T(8,128)(2,1)} %get-tuple-element.12) | data formatting | bytes 10485760 | tf_op jit(solution)/shard_map/reshape;squeeze | solution.py:54
  175.4 14.8 %all-gather.5.cloned.1.call-done = bf16[3,128,4096]{2,1,0:T(8,128)(2,1)} async-done(((bf16[3,128,256]{2,1,0:T(8,128)(2,1)}), bf16[3,128,4096]{2,1,0:T(8,128)(2,1)}) %all-gather.5.cloned.1.call-update) | async-done | bytes 3145744 | tf_op jit(solution)/shard_map/all_gather | solution.py:75
  190.2 4.3 %convolution_bitcast_fusion = f32[2,640,128]{2,1,0:T(8,128)S(1)} fusion(bf16[3,128,4096]{2,1,0:T(8,128)(2,1)} %all-gather.5.cloned.1.call-done, bf16[640,4096,1]{1,0,2:T(8,128)(2,1)} %reshape.46), kind=kOutput, calls=%fused_computation.11 | convolution fusion | flops 1342177280 | bytes 9043968 | tf_op jit(solution)/shard_map/rd,gfd->grf/dot_general | solution.py:76
  194.6 4.4 %fusion.21 = (bf16[1,640,128]{2,1,0:T(8,128)(2,1)S(1)}, bf16[1,640,128]{2,1,0:T(8,128)(2,1)S(1)}) fusion(f32[2,640,128]{2,1,0:T(8,128)S(1)} %convolution_bitcast_fusion, bf16[640,4096]{1,0:T(8,128)(2,1)} %reshape_squeeze.6, bf16[3,128,4096]{2,1,0:T(8,128)(2,1)} %all-gather.5.cloned.1.call-done), kind=kOutput, calls=%fused_computation.53 | convolution fusion | flops 672153600 | bytes 7274496 | tf_op jit(solution)/shard_map/rd,fd->rf/dot_general | solution.py:79
  199.0 3.2 %convolution_convert_fusion = bf16[2,128,4096]{2,1,0:T(8,128)(2,1)} fusion(bf16[640,4096,1]{1,0,2:T(8,128)(2,1)S(1)} %bitcast.77, bf16[1,640,128]{2,1,0:T(8,128)(2,1)S(1)} %get-tuple-element.15, bf16[1,640,128]{2,1,0:T(8,128)(2,1)S(1)} %get-tuple-element.14), kind=kOutput, calls=%fused_computation.2 | convolution fusion | flops 1343389696 | bytes 7667712 | tf_op jit(solution)/shard_map/grf,rd->gfd/dot_general | solution.py:91
  202.2 67.5 %reduce-scatter.2.cloned.1.call-done = bf16[2,128,256]{2,1,0:T(8,128)(2,1)} async-done(((bf16[2,128,4096]{2,1,0:T(8,128)(2,1)}), bf16[2,128,256]{2,1,0:T(8,128)(2,1)}) %reduce-scatter.2.cloned.1.call-update) | async-done | bytes 131088 | tf_op jit(solution)/shard_map/reduce_scatter | solution.py:94
  269.8 9.3 %collective-permute-start.1 = (bf16[2,128,256]{2,1,0:T(8,128)(2,1)}, bf16[2,128,256]{2,1,0:T(8,128)(2,1)S(1)}, u32[]{:S(2)}, u32[]{:S(2)}) collective-permute-start(bf16[2,128,256]{2,1,0:T(8,128)(2,1)} %reduce-scatter.2.cloned.1.call-done), channel_id=1, source_target_pairs={{0,0},{1,128},{2,256},{3,384},{128,1},{129,129},{130,257},{131,385... | collective-permute-start | bytes 393224 | tf_op jit(solution)/shard_map/ppermute | solution.py:97
  279.1 8.1 %collective-permute-done.1 = bf16[2,128,256]{2,1,0:T(8,128)(2,1)S(1)} collective-permute-done((bf16[2,128,256]{2,1,0:T(8,128)(2,1)}, bf16[2,128,256]{2,1,0:T(8,128)(2,1)S(1)}, u32[]{:S(2)}, u32[]{:S(2)}) %collective-permute-start.1) | collective-permute-done | bytes 131104 | tf_op jit(solution)/shard_map/ppermute | solution.py:97
  287.2 15.5 %all_to_all.34 = bf16[2,128,256]{1,0,2:T(2,128)(2,1)S(1)} all-to-all(bf16[2,128,256]{1,0,2:T(2,128)(2,1)S(1)} %copy.113), channel_id=1, replica_groups=mesh['y'=4,'zl'=4,'c'=2,'x'=4,'zh'=4] {'c'}, dimensions={2} | all-to-all | bytes 262144 | tf_op jit(solution)/shard_map/all_to_all | solution.py:98
  302.9 0.2 reshape.42
  303.2 0.4 bitcast_reduce_fusion
  303.6 0.8 copy.115
  304.4 0.6 broadcast_multiply_fusion
  (43 shorter events, 1.8 us)
Async XLA Ops:
  7.2 3.5 %copy-start = (bf16[256,4096]{1,0:T(8,128)(2,1)S(1)}, bf16[256,4096]{1,0:T(8,128)(2,1)}, u32[]{:S(2)}) copy-start(bf16[256,4096]{1,0:T(8,128)(2,1)} %param.8) | copy-start | bytes 6291460
  7.2 99.5 %all-gather.3.cloned.1.call-start = ((), (), s32[]{:S(2)}) async-start(), calls=%async_computation.4 | async-start | bytes 11796480 | tf_op jit(solution)/shard_map/all_gather | solution.py:50
  9.6 1.6 copy-start.1
  11.9 22.5 %copy-start.2 = (s32[2,256,128]{2,1,0:T(8,128)S(1)}, s32[2,256,128]{2,1,0:T(8,128)}, u32[]{:S(2)}) copy-start(s32[2,256,128]{2,1,0:T(8,128)} %param.12) | copy-start | bytes 786436
  11.9 22.7 %copy-start.6 = (f32[8,128]{1,0:T(8,128)S(1)}, f32[8,128]{1,0:T(8,128)}, u32[]{:S(2)}) copy-start(f32[8,128]{1,0:T(8,128)} %param.15) | copy-start | bytes 12292
  13.3 21.4 %copy-start.4 = (s32[256,128]{1,0:T(8,128)S(1)}, s32[256,128]{1,0:T(8,128)}, u32[]{:S(2)}) copy-start(s32[256,128]{1,0:T(8,128)} %param.14) | copy-start | bytes 393220
  13.3 21.5 %copy-start.5 = (f32[2,256,4]{1,2,0:T(4,128)S(1)}, f32[2,256,4]{1,2,0:T(4,128)}, u32[]{:S(2)}) copy-start(f32[2,256,4]{1,2,0:T(4,128)} %param.13) | copy-start | bytes 24580
  34.4 155.8 %all-gather.5.cloned.1.call-start = ((), (), s32[]{:S(2)}) async-start(), calls=%async_computation.5 | async-start | bytes 3342336 | tf_op jit(solution)/shard_map/all_gather | solution.py:75
  41.5 20.4 %collective-permute-start = (bf16[3,128,256]{2,1,0:T(8,128)(2,1)S(1)}, bf16[3,128,256]{2,1,0:T(8,128)(2,1)S(1)}, u32[]{:S(2)}, u32[]{:S(2)}) collective-permute-start(bf16[3,128,256]{2,1,0:T(8,128)(2,1)S(1)} %all_to_all.27), channel_id=1, source_target_pairs={{0,0},{1,128},{2,256},{3,384},{128,1},{129,129},{130,257},{131,385... | collective-permute-start | bytes 589832 | tf_op jit(solution)/shard_map/ppermute | solution.py:74
  61.8 0.7 copy-start.3
  62.5 207.2 %reduce-scatter.2.cloned.1.call-start = ((), (), s32[]{:S(2)}) async-start(), calls=%async_computation.6 | async-start | bytes 2228224 | tf_op jit(solution)/shard_map/reduce_scatter | solution.py:94
  190.2 8.7 %slice-start = ((s8[5242880]{0:T(1024)(128)(4,1)}), s8[4194304]{0:T(1024)(128)(4,1)S(1)}, s32[]{:S(2)}) async-start(s8[5242880]{0:T(1024)(128)(4,1)} %bitcast.76), calls=%async_computation.7 | async-start | bytes 8388608
  194.5 4.4 %slice-start.1 = ((s8[5242880]{0:T(1024)(128)(4,1)}), s8[1048576]{0:T(1024)(128)(4,1)S(1)}, s32[]{:S(2)}) async-start(s8[5242880]{0:T(1024)(128)(4,1)} %bitcast.76), calls=%async_computation.8 | async-start | bytes 2097152
  269.8 17.3 %collective-permute-start.1 = (bf16[2,128,256]{2,1,0:T(8,128)(2,1)}, bf16[2,128,256]{2,1,0:T(8,128)(2,1)S(1)}, u32[]{:S(2)}, u32[]{:S(2)}) collective-permute-start(bf16[2,128,256]{2,1,0:T(8,128)(2,1)} %reduce-scatter.2.cloned.1.call-done), channel_id=1, source_target_pairs={{0,0},{1,128},{2,256},{3,384},{128,1},{129,129},{130,257},{131,385... | collective-permute-start | bytes 393224 | tf_op jit(solution)/shard_map/ppermute | solution.py:97
Sparse Core Ops, SparseCore 0:
  34.5 72.1 all-gather.2
  109.3 80.8 all-gather.4
  202.4 67.3 reduce-scatter.1

commit v2 on v0

v2 whole, which is shorter than its diff:
```python
import jax
import jax.numpy as jnp
from jax import lax
from jax.experimental import pallas as pl
from jax.experimental.pallas import tpu as pltpu
from jax.sharding import PartitionSpec as P

BLOCK = 32
CAP = 20
NX, NY, NZ, NC = 4, 4, 16, 2
SEG = 4
POOL = NY * NC
D = 4096
TOK = 256
MAIN = 16
TAIL = CAP - MAIN
QUART = D // SEG
PACK = D + QUART
HID = 256
SUB = HID // POOL
FEAT = 128
PIECE = 3 * SUB
HALF = PIECE // 2
PMAIN = POOL * MAIN
PTAIL = POOL * TAIL
ROWS = NX * PMAIN
TAILS = NX * PTAIL
WIDTH = SEG * SUB
OFFSETS = (0, 1, 3, 2)
STEPS = NZ // 2
MESH = pl.DeviceIdType.MESH
LSQ = 192.0 ** (-0.5)
F32 = jnp.float32
BF16 = jnp.bfloat16


def decode_values(code_array):
    modulus = (code_array % 8).astype(F32)
    levels = jnp.where(
        modulus < 4.0,
        0.5 * modulus,
        jnp.where(modulus < 6.0, modulus - 2.0, jnp.where(modulus < 7.0, 4.0, 6.0)),
    )
    return jnp.where(code_array >= 8, -levels, levels)


def iota(shape, axis):
    return lax.broadcasted_iota(jnp.int32, shape, axis)


def nt_dot(a, b):
    return lax.dot_general(a, b, (((1,), (1,)), ((), ())), preferred_element_type=F32)


def dot(a, b):
    return jnp.dot(a, b, preferred_element_type=F32)


def device_at(x, y, z, c):
    return (y * (SEG * NC) + lax.rem(z, SEG) * NC + c, x * SEG + z // SEG)


def kernel(
    tok_hbm,
    cot_hbm,
    routes_ref,
    combine_ref,
    gu_codes_ref,
    gu_scales_ref,
    d_codes_ref,
    d_scales_ref,
    grad_ref,
    scale_ref,
    tok_v,
    cot_v,
    sbuf,
    xbuf,
    xtail,
    wsend,
    wfull,
    pre_tail,
    g_t,
    dw,
    rs_out,
    rs_in,
    fin_out,
    fin_in,
    load_sem,
    x_s,
    x_r,
    y_s,
    y_r,
    p_s,
    p_r,
    a_s,
    a_r,
    w_s,
    w_r,
    r_s,
    r_r,
    f_s,
    f_r,
):
    dp = lax.axis_index("dp")
    tensor = lax.axis_index("tensor")
    x, zh = tensor // SEG, lax.rem(tensor, SEG)
    y, rest = dp // (SEG * NC), lax.rem(dp, SEG * NC)
    zl, c = rest // NC, lax.rem(rest, NC)
    z = zh * SEG + zl
    p = y * NC + c
    oc = 1 - c
    y_up, y_dn, y_far = lax.rem(y + 1, NY), lax.rem(y + NY - 1, NY), lax.rem(y + 2, NY)
    z_up, z_dn = lax.rem(z + 1, NZ), lax.rem(z + NZ - 1, NZ)
    to_y = (device_at(x, y_up, z, c), device_at(x, y_dn, z, c))
    to_z = (device_at(x, y, z_up, c), device_at(x, y, z_dn, c))
    partner = device_at(x, y, z, oc)

    def member(index):
        return device_at(x, index // NC, z, lax.rem(index, NC))

    def copy(src, dst, sent, got, device):
        return pltpu.make_async_remote_copy(
            src_ref=src,
            dst_ref=dst,
            send_sem=sent,
            recv_sem=got,
            device_id=device,
            device_id_type=MESH,
        )

    started = []

    def send(src, dst, sent, got, device):
        one = copy(src, dst, sent, got, device)
        one.start()
        started.append(one)

    def arrived(dst, sent, got):
        copy(dst, dst, sent, got, partner).wait_recv()

    loads = [
        pltpu.make_async_copy(tok_hbm, tok_v, load_sem.at[0]),
        pltpu.make_async_copy(cot_hbm, cot_v, load_sem.at[1]),
    ]
    for one in loads:
        one.start()

    barrier = pltpu.get_barrier_semaphore()
    peers = [member(lax.rem(p + k, POOL)) for k in range(1, POOL)]
    peers += [device_at(lax.rem(x + o, NX), y, z, c) for o in range(1, NX)]
    peers += list(to_z)
    for peer in peers:
        pl.semaphore_signal(barrier, inc=1, device_id=peer, device_id_type=MESH)

    lane_block = iota((HID, FEAT), 1) // BLOCK
    for g in range(2):
        rows = pl.ds(g * HID, HID)
        scale = jnp.zeros((HID, FEAT), F32)
        for b in range(FEAT // BLOCK):
            scale = jnp.where(lane_block == b, gu_scales_ref[rows, b : b + 1], scale)
        weight = (scale * decode_values(gu_codes_ref[rows, :])).astype(BF16)
        for m in range(POOL):
            wsend[m, g * SUB : (g + 1) * SUB, :] = weight[m * SUB : (m + 1) * SUB, :]
    for m in range(POOL):
        values = decode_values(d_codes_ref[m * SUB : (m + 1) * SUB, :])
        wsend[m, 2 * SUB : 3 * SUB, :] = (d_scales_ref[m : m + 1, :] * values).astype(BF16)

    pl.semaphore_wait(barrier, len(peers))

    def piece(origin, first=0, count=PIECE):
        row = pl.multiple_of((origin // SEG) * PIECE + first, 16)
        column = pl.multiple_of(lax.rem(origin, SEG) * QUART, QUART)
        return wfull.at[pl.ds(row, count), pl.ds(column, QUART)]

    def part(index):
        row = pl.multiple_of(zh * PIECE, 16)
        column = pl.multiple_of(zl * QUART + index * FEAT, FEAT)
        return wfull.at[pl.ds(row, PIECE), pl.ds(column, FEAT)]

    own_part = pltpu.make_async_copy(wsend.at[p], part(p), load_sem.at[2])
    own_part.start()
    for k in range(1, POOL):
        to = lax.rem(p + k, POOL)
        send(wsend.at[to], part(p), a_s.at[k - 1], a_r.at[k - 1], member(to))

    masks, weights = [], []
    for e in range(NX):
        chosen = routes_ref[...] == e
        masks.append(jnp.max(chosen.astype(F32), axis=0, keepdims=True))
        weights.append(
            jnp.sum(jnp.where(chosen, combine_ref[...], 0.0), axis=0, keepdims=True)
        )
    mask = jnp.concatenate(masks + [jnp.zeros((4, TOK), F32)], axis=0)
    before = (iota((TOK, TOK), 0) <= iota((TOK, TOK), 1)).astype(F32).astype(BF16)
    count = dot(mask.astype(BF16), before)
    place = jnp.where(mask > 0.0, count - 1.0, -1.0).astype(jnp.int32)
    wide = (MAIN, TOK)
    place = jnp.concatenate(
        [jnp.broadcast_to(place[e : e + 1], wide) for e in range(NX)], axis=0
    )
    weight = jnp.concatenate(
        [jnp.broadcast_to(weights[e], wide) for e in range(NX)], axis=0
    )
    slot = lax.rem(iota((NX * MAIN, TOK), 0), MAIN)
    is_main = place == slot
    is_tail = place == MAIN + lax.rem(slot, TAIL)
    main_weight = jnp.sum(jnp.where(is_main, weight, 0.0), axis=1, keepdims=True)
    tail_weight = jnp.sum(jnp.where(is_tail, weight, 0.0), axis=1, keepdims=True)
    pick_main = is_main.astype(F32).astype(BF16)
    pick_tail = [
        (is_tail & (slot // TAIL == k)).astype(F32).astype(BF16) for k in range(SEG)
    ]
    wide = QUART // NY
    for which, (source, load) in enumerate(zip((tok_v, cot_v), loads)):
        load.wait()
        for quarter in range(NY):
            folded = jnp.zeros((NX * MAIN, wide), F32)
            for k in range(SEG):
                first = quarter * QUART + k * wide
                values = source[:, first : first + wide]
                picked = dot(pick_main, values)
                folded = folded + dot(pick_tail[k], values)
                if which == 1:
                    picked = picked * main_weight
                to = k * QUART + quarter * wide
                sbuf[which, :, to : to + wide] = picked.astype(BF16)
            if which == 1:
                folded = folded * tail_weight
            to = D + quarter * wide
            sbuf[which, :, to : to + wide] = folded.astype(BF16)

    def for_expert(e):
        return sbuf.at[:, pl.ds(pl.multiple_of(e * MAIN, MAIN), MAIN), :]

    def rows_of(group, at_y, at_c):
        row = group * PMAIN + (at_y * NC + at_c) * MAIN
        return pl.ds(pl.multiple_of(row, MAIN), MAIN)

    def block(group, at_y, at_c):
        return xbuf.at[:, rows_of(group, at_y, at_c), :]

    def one_block(which, group, at_y, at_c):
        return xbuf.at[which, rows_of(group, at_y, at_c), :]

    own_rows = pltpu.make_async_copy(for_expert(x), block(0, y, c), load_sem.at[3])
    own_rows.start()
    for group in range(1, NX):
        e = lax.rem(x + OFFSETS[group], NX)
        send(
            for_expert(e),
            block(group, y, c),
            x_s.at[group - 1],
            x_r.at[group - 1],
            device_at(e, y, z, c),
        )

    def spread(group):
        if group == 0:
            source = for_expert(x)
        else:
            source = block(group, y, c)
            arrived(source, x_s.at[group - 1], x_r.at[group - 1])
        for way in range(2):
            send(
                source,
                block(group, y, c),
                y_s.at[0, way, group],
                y_r.at[0, way, group],
                to_y[way],
            )
        send(source, block(group, y, c), p_s.at[group, 0], p_r.at[group, 0], partner)

    def relay(group):
        for way in range(2):
            from_y = (y_dn, y_up)[way]
            whole = block(group, from_y, c)
            arrived(whole, y_s.at[0, way, group], y_r.at[0, way, group])
            half = one_block(way, group, from_y, c)
            send(half, half, y_s.at[1, way, group], y_r.at[1, way, group], to_y[way])
            send(whole, whole, p_s.at[group, 1 + way], p_r.at[group, 1 + way], partner)

    def relay_far(group):
        for way in range(2):
            half = one_block(way, group, y_far, c)
            arrived(half, y_s.at[1, way, group], y_r.at[1, way, group])
            send(half, half, p_s.at[group, 3 + way], p_r.at[group, 3 + way], partner)

    def all_rows(group):
        arrived(block(group, y, oc), p_s.at[group, 0], p_r.at[group, 0])
        arrived(block(group, y_dn, oc), p_s.at[group, 1], p_r.at[group, 1])
        arrived(block(group, y_up, oc), p_s.at[group, 2], p_r.at[group, 2])
        for way in range(2):
            half = one_block(way, group, y_far, oc)
            arrived(half, p_s.at[group, 3 + way], p_r.at[group, 3 + way])

    def weight_piece(step, way, origin):
        if step < STEPS:
            return piece(origin)
        return piece(origin, way * HALF, HALF)

    def weights_on(step):
        for way in range(2):
            back = NZ - (step - 1) if way == 0 else step - 1
            ref = weight_piece(step, way, lax.rem(z + back, NZ))
            send(ref, ref, w_s.at[way, step - 1], w_r.at[way, step - 1], to_z[way])

    def weights_in(step):
        for way in range(2):
            back = NZ - step if way == 0 else step
            ref = weight_piece(step, way, lax.rem(z + back, NZ))
            arrived(ref, w_s.at[way, step - 1], w_r.at[way, step - 1])
        if step < STEPS:
            weights_on(step + 1)

    spread(0)
    own_part.wait()
    for k in range(1, POOL):
        got = part(lax.rem(p + POOL - k, POOL))
        arrived(got, a_s.at[k - 1], a_r.at[k - 1])
    weights_on(1)

    weights_in(1)
    relay(0)
    weights_in(2)
    spread(1)
    spread(2)
    relay_far(0)
    weights_in(3)
    spread(3)
    relay(1)
    weights_in(4)
    relay_far(1)
    own_rows.wait()

    fold_from = iota((PMAIN, PMAIN), 1)
    fold_to = iota((PMAIN, PMAIN), 0)
    inside = lax.rem(fold_to, PTAIL)
    wanted = (inside // TAIL) * MAIN + (fold_to // PTAIL) * TAIL + lax.rem(inside, TAIL)
    unfold = (fold_from == wanted).astype(F32).astype(BF16)

    def unpack(group):
        all_rows(group)
        for which in range(2):
            folded = xbuf[which, group * PMAIN : (group + 1) * PMAIN, D:PACK]
            tails = dot(unfold, folded).astype(BF16)
            for k in range(SEG):
                xtail[
                    which,
                    group * PTAIL : (group + 1) * PTAIL,
                    k * QUART : (k + 1) * QUART,
                ] = tails[k * PTAIL : (k + 1) * PTAIL, :]

    def gradients(gate, up, back):
        sig = jax.nn.sigmoid(gate)
        to_gate = back * up * sig * (1.0 + gate * (1.0 - sig))
        to_up = back * (gate * sig)
        return to_gate.T.astype(BF16), to_up.T.astype(BF16)

    depth = 512

    def forward(group):
        rows = pl.ds(group * PMAIN, PMAIN)
        tails = pl.ds(group * PTAIL, PTAIL)

        def one(step, total):
            columns = pl.ds(pl.multiple_of(step * depth, depth), depth)

            def side(kind):
                return [
                    wfull[q * PIECE + kind * SUB : q * PIECE + (kind + 1) * SUB, columns]
                    for q in range(SEG)
                ]

            gate_up = jnp.concatenate(side(0) + side(1), axis=0)
            down = jnp.concatenate(side(2), axis=0)
            tokens = jnp.concatenate([xbuf[0, rows, columns], xtail[0, tails, columns]], 0)
            scaled = jnp.concatenate([xbuf[1, rows, columns], xtail[1, tails, columns]], 0)
            return total[0] + nt_dot(tokens, gate_up), total[1] + nt_dot(scaled, down)

        count = PMAIN + PTAIL
        start = (jnp.zeros((count, 2 * WIDTH), F32), jnp.zeros((count, WIDTH), F32))
        front, back = lax.fori_loop(0, D // depth, one, start)
        to_gate, to_up = gradients(
            front[:PMAIN, :WIDTH], front[:PMAIN, WIDTH:], back[:PMAIN]
        )
        g_t[:WIDTH, rows] = to_gate
        g_t[WIDTH:, rows] = to_up
        pre_tail[tails, : 2 * WIDTH] = front[PMAIN:]
        pre_tail[tails, 2 * WIDTH :] = back[PMAIN:]

    weights_in(5)
    relay(2)
    unpack(0)
    weights_in(6)
    relay_far(2)
    unpack(1)
    weights_in(7)
    relay(3)
    unpack(2)
    weights_in(8)
    forward(0)
    relay_far(3)
    forward(1)
    forward(2)
    unpack(3)
    forward(3)
    to_gate, to_up = gradients(
        pre_tail[:, :WIDTH], pre_tail[:, WIDTH : 2 * WIDTH], pre_tail[:, 2 * WIDTH :]
    )
    g_t[:WIDTH, ROWS:] = to_gate
    g_t[WIDTH:, ROWS:] = to_up

    wide_out = 256

    def weight_gradient(turn):
        at = lax.rem(zl + turn, SEG)

        def one(step, carry):
            first = pl.multiple_of(at * QUART + step * wide_out, wide_out)
            total = dot(g_t[:, :ROWS], xbuf[0, :, pl.ds(first, wide_out)])
            total = total + dot(g_t[:, ROWS:], xtail[0, :, pl.ds(first, wide_out)])
            to = pl.ds(pl.multiple_of(step * wide_out, wide_out), wide_out)
            dw[at, :, to] = total
            return carry

        lax.fori_loop(0, QUART // wide_out, one, 0)

    def own_term(dest, kind):
        row = pl.multiple_of(kind * WIDTH + (dest // SEG) * SUB, SUB)
        return dw[lax.rem(dest, SEG), pl.ds(row, SUB), :]

    def sum_in(step, way, kind):
        ref = rs_in.at[way, step, kind]
        arrived(ref, r_s.at[way, step, kind], r_r.at[way, step, kind])
        return rs_in[way, step, kind].astype(F32)

    def sum_on(step):
        for kind in range(2):
            for way in range(2):
                if step == 0 and kind != way:
                    continue
                ahead = STEPS - step if way == 0 else NZ - STEPS + step
                total = own_term(lax.rem(z + ahead, NZ), kind)
                if step > 1 or (step == 1 and kind == way):
                    total = total + sum_in(step - 1, way, kind)
                rs_out[way, step, kind] = total.astype(BF16)
                send(
                    rs_out.at[way, step, kind],
                    rs_in.at[way, step, kind],
                    r_s.at[way, step, kind],
                    r_r.at[way, step, kind],
                    to_z[way],
                )

    weight_gradient(0)
    sum_on(0)
    weight_gradient(1)
    weight_gradient(3)
    sum_on(1)
    weight_gradient(2)
    for step in range(2, STEPS):
        sum_on(step)

    for kind in range(2):
        total = own_term(z, kind)
        for way in range(2):
            total = total + sum_in(STEPS - 1, way, kind)
        total = total.astype(BF16)
        for m in range(POOL):
            fin_out[m, kind * SUB : (kind + 1) * SUB, :] = total[
                :, m * FEAT : (m + 1) * FEAT
            ]
    own_sum = pltpu.make_async_copy(fin_out.at[p], fin_in.at[p], load_sem.at[4])
    own_sum.start()
    for k in range(1, POOL):
        to = lax.rem(p + k, POOL)
        send(fin_out.at[to], fin_in.at[p], f_s.at[k - 1], f_r.at[k - 1], member(to))
    own_sum.wait()
    for k in range(1, POOL):
        arrived(fin_in.at[lax.rem(p + POOL - k, POOL)], f_s.at[k - 1], f_r.at[k - 1])

    to_block = (iota((FEAT, FEAT), 0) // BLOCK == iota((FEAT, FEAT), 1)).astype(F32)
    for kind in range(2):
        summed = jnp.concatenate(
            [fin_in[m, kind * SUB : (kind + 1) * SUB, :] for m in range(POOL)], axis=0
        ).astype(F32)
        codes = gu_codes_ref[kind * HID : (kind + 1) * HID, :]
        grad_ref[kind * HID : (kind + 1) * HID, :] = jnp.where(codes % 8 != 7, summed, 0.0)
        blocks = jnp.dot(
            summed * decode_values(codes),
            to_block,
            precision=lax.Precision.HIGHEST,
            preferred_element_type=F32,
        )
        scale_ref[kind * HID : (kind + 1) * HID, :] = LSQ * blocks[:, : FEAT // BLOCK]
    for one in started:
        one.wait_send()


def body(tokens, cotangent, routes, combine, gu_codes, gu_scales, d_codes, d_scales):
    hidden, width = gu_codes.shape[1], gu_codes.shape[2]
    vmem = pl.BlockSpec(memory_space=pltpu.VMEM)
    hbm = pl.BlockSpec(memory_space=pl.ANY)
    dma = pltpu.SemaphoreType.DMA
    grad, scale = pl.pallas_call(
        kernel,
        out_shape=(
            jax.ShapeDtypeStruct((2 * hidden, width), F32),
            jax.ShapeDtypeStruct((2 * hidden, width // BLOCK), F32),
        ),
        in_specs=[hbm, hbm] + [vmem] * 6,
        out_specs=(vmem, vmem),
        scratch_shapes=[
            pltpu.VMEM((TOK, D), BF16),
            pltpu.VMEM((TOK, D), BF16),
            pltpu.VMEM((2, NX * MAIN, PACK), BF16),
            pltpu.VMEM((2, ROWS, PACK), BF16),
            pltpu.VMEM((2, TAILS, D), BF16),
            pltpu.VMEM((POOL, PIECE, FEAT), BF16),
            pltpu.VMEM((SEG * PIECE, D), BF16),
            pltpu.VMEM((TAILS, 3 * WIDTH), F32),
            pltpu.VMEM((2 * WIDTH, ROWS + TAILS), BF16),
            pltpu.VMEM((SEG, 2 * WIDTH, QUART), F32),
            pltpu.VMEM((2, STEPS, 2, SUB, QUART), BF16),
            pltpu.VMEM((2, STEPS, 2, SUB, QUART), BF16),
            pltpu.VMEM((POOL, 2 * SUB, FEAT), BF16),
            pltpu.VMEM((POOL, 2 * SUB, FEAT), BF16),
            dma((5,)),
            dma((NX - 1,)),
            dma((NX - 1,)),
            dma((2, 2, NX)),
            dma((2, 2, NX)),
            dma((NX, 5)),
            dma((NX, 5)),
            dma((POOL - 1,)),
            dma((POOL - 1,)),
            dma((2, STEPS)),
            dma((2, STEPS)),
            dma((2, STEPS, 2)),
            dma((2, STEPS, 2)),
            dma((POOL - 1,)),
            dma((POOL - 1,)),
        ],
        compiler_params=pltpu.CompilerParams(
            collective_id=0, has_side_effects=True, vmem_limit_bytes=56 << 20
        ),
        cost_estimate=pl.CostEstimate(
            flops=2 * 640 * D * 5 * WIDTH, bytes_accessed=8 << 20, transcendentals=0
        ),
    )(
        tokens,
        cotangent,
        routes.T,
        combine.T,
        gu_codes.reshape(2 * hidden, width),
        gu_scales.reshape(2 * hidden, width // BLOCK),
        d_codes,
        d_scales,
    )
    return (
        grad.reshape(2, hidden, width),
        scale.reshape(2, hidden, width // BLOCK),
    )


def solution(mesh):
    rows = P(("dp", "tensor"), None)
    return jax.shard_map(
        body,
        mesh=mesh,
        in_specs=(
            rows,
            rows,
            rows,
            rows,
            P(None, "tensor", "dp"),
            P(None, "tensor", "dp"),
            P("tensor", "dp"),
            P("tensor", "dp"),
        ),
        out_specs=(P(None, "tensor", "dp"), P(None, "tensor", "dp")),
        check_vma=False,
    )
```

time: 543 us -> 130 us (0.24)
  waiting for transfers between devices: 444 us -> 0 us
  Pallas kernels: 0 us -> 124 us
  starting transfers between devices: 28.5 us -> 0 us
  local copies, waits for them, and re-layouts: 30.4 us -> 4.88 us
  matrix products: 14.2 us -> 0 us
  between operations: 14.2 us -> 0.64 us
  other arithmetic: 6 us -> 0 us
    all_to_all x2 -> x0, waiting for transfers between devices: 293 us -> none  [the longest x1 160 us: body(): lax.all_to_all(send_tokens, 'tensor', split_axis=0, concat_axis=0, tiled=...]
    unnamed x3 -> x0, waiting for transfers between devices: 152 us -> none
    pallas_call x0 -> x1, Pallas kernels: none -> 124 us  [body(): pl.pallas_call(kernel, out_shape=(jax.ShapeDtypeStruct((2 * hidden, width...]
    all_to_all x2 -> x0, starting transfers between devices: 28.5 us -> none  [the longest x1 18.4 us: body(): lax.all_to_all(send_scaled, 'tensor', split_axis=0, concat_axis=0, tiled=...]
    dot_general x5 -> x0, matrix products: 14.2 us -> none  [the longest x1 4.7 us: body(): jnp.einsum('rd,gfd->grf', token_rows, gathered[:2], preferred_element_typ...]
    unnamed x19 -> x3, local copies, waits for them, and re-layouts: 17.1 us -> 4.88 us
    reshape x2 -> x0, local copies, waits for them, and re-layouts: 8.64 us -> none  [the longest x1 4.35 us: body(): token_rows = token_block.reshape(-1, width_full)]
  transfers between devices with their start and end apart: 4 -> 0, of which waited for: 3 -> 0; matrix products, arithmetic and copies ran while one was open for 3% -> 0% of each run, Pallas kernels for 0% -> 0%
where the time goes in v2:
time: 130 us
  Pallas kernels  124 us (95%)
  local copies, waits for them, and re-layouts  4.88 us (4%)
    pallas_call x1, Pallas kernels, body(): pl.pallas_call(kernel, out_shape=(jax.ShapeDtypeStruct((2 * hidden, width...  124 us
    unnamed x3, local copies, waits for them, and re-layouts  4.88 us

profile of v2, /device:TPU:1, one launch (start us, length us, event | category | flops | bytes accessed | tf_op | source)
XLA Modules:
  0.0 129.8 jit_solution(12664369076392119654)
XLA Ops:
  0.6 1.6 %copy.10 = f32[2,256,4]{2,1,0:T(8,128)} copy(f32[2,256,4]{1,2,0:T(4,128)} %param.13) | data formatting | bytes 16384 | tf_op args[5]
  2.2 124.3 %shard_map.95 = (f32[512,128]{1,0:T(8,128)}, f32[512,4]{1,0:T(8,128)}) custom-call(bf16[256,4096]{1,0:T(8,128)(2,1)} %tok_hbm.1, bf16[256,4096]{1,0:T(8,128)(2,1)} %cot_hbm.1, s32[8,256]{1,0:T(8,128)} %bitcast.10, f32[8,256]{1,0:T(8,128)} %bitcast.11, s32[512,128]{1,0:T(8,128)} %bitcast.9, f32[512,4]{1,0:T(8,128)} %bitcast.8, s32[256,128]{1,0:T(8,128)} %d_codes_ref.1, ...), custom_call_target="tpu_custom_call" | custom-call | flops 3355443200 | bytes 8388608 | tf_op jit(solution)/shard_map/pallas_call | solution.py:505
  126.5 1.7 %copy.11 = f32[2,256,4]{1,2,0:T(4,128)} copy(f32[2,256,4]{2,1,0:T(8,128)} %bitcast.7) | data formatting | bytes 16384
  128.2 1.7 %copy.13 = f32[2,256,128]{2,1,0:T(8,128)} copy(f32[2,256,128]{2,1,0:T(8,128)} %bitcast.6) | data formatting | bytes 524288

commit v3 on v2

v3 whole, which is shorter than its diff:
```python
import jax
import jax.numpy as jnp
from jax import lax
from jax.experimental import pallas as pl
from jax.experimental.pallas import tpu as pltpu
from jax.sharding import PartitionSpec as P

BLOCK = 32
CAP = 20
NX, NY, NZ, NC = 4, 4, 16, 2
SEG = 4
POOL = NY * NC
D = 4096
TOK = 256
MAIN = 16
TAIL = CAP - MAIN
QUART = D // SEG
PACK = D + QUART
HID = 256
SUB = HID // POOL
FEAT = 128
PIECE = 3 * SUB
HALF = PIECE // 2
PMAIN = POOL * MAIN
PTAIL = POOL * TAIL
ROWS = NX * PMAIN
TAILS = NX * PTAIL
WIDTH = SEG * SUB
OFFSETS = (0, 1, 3, 2)
STEPS = NZ // 2
PART = QUART // NY
MESH = pl.DeviceIdType.MESH
LSQ = 192.0 ** (-0.5)
F32 = jnp.float32
BF16 = jnp.bfloat16


def decode_values(code_array):
    modulus = (code_array % 8).astype(F32)
    levels = jnp.where(
        modulus < 4.0,
        0.5 * modulus,
        jnp.where(modulus < 6.0, modulus - 2.0, jnp.where(modulus < 7.0, 4.0, 6.0)),
    )
    return jnp.where(code_array >= 8, -levels, levels)


def iota(shape, axis):
    return lax.broadcasted_iota(jnp.int32, shape, axis)


def nt_dot(a, b):
    return lax.dot_general(a, b, (((1,), (1,)), ((), ())), preferred_element_type=F32)


def dot(a, b):
    return jnp.dot(a, b, preferred_element_type=F32)


def device_at(x, y, z, c):
    return (y * (SEG * NC) + lax.rem(z, SEG) * NC + c, x * SEG + z // SEG)


def kernel(
    tok_hbm,
    cot_hbm,
    routes_hbm,
    combine_hbm,
    gu_codes_hbm,
    gu_scales_hbm,
    d_codes_hbm,
    d_scales_hbm,
    grad_ref,
    scale_ref,
    tok_v,
    cot_v,
    routes_ref,
    combine_ref,
    gu_codes_ref,
    gu_scales_ref,
    d_codes_ref,
    d_scales_ref,
    sbuf,
    xbuf,
    xtail,
    wsend,
    wfull,
    pre_tail,
    g_t,
    dw,
    rs_out,
    rs_in,
    fin_out,
    fin_in,
    load_sem,
    x_s,
    x_r,
    y_s,
    y_r,
    p_s,
    p_r,
    a_s,
    a_r,
    w_s,
    w_r,
    r_s,
    r_r,
    f_s,
    f_r,
):
    dp = lax.axis_index("dp")
    tensor = lax.axis_index("tensor")
    x, zh = tensor // SEG, lax.rem(tensor, SEG)
    y, rest = dp // (SEG * NC), lax.rem(dp, SEG * NC)
    zl, c = rest // NC, lax.rem(rest, NC)
    z = zh * SEG + zl
    p = y * NC + c
    oc = 1 - c
    y_up, y_dn, y_far = lax.rem(y + 1, NY), lax.rem(y + NY - 1, NY), lax.rem(y + 2, NY)
    z_up, z_dn = lax.rem(z + 1, NZ), lax.rem(z + NZ - 1, NZ)
    to_y = (device_at(x, y_up, z, c), device_at(x, y_dn, z, c))
    to_z = (device_at(x, y, z_up, c), device_at(x, y, z_dn, c))
    partner = device_at(x, y, z, oc)

    def member(index):
        return device_at(x, index // NC, z, lax.rem(index, NC))

    def copy(src, dst, sent, got, device):
        return pltpu.make_async_remote_copy(
            src_ref=src,
            dst_ref=dst,
            send_sem=sent,
            recv_sem=got,
            device_id=device,
            device_id_type=MESH,
        )

    started = []

    def send(src, dst, sent, got, device):
        one = copy(src, dst, sent, got, device)
        one.start()
        started.append(one)

    def arrived(dst, sent, got):
        copy(dst, dst, sent, got, partner).wait_recv()

    barrier = pltpu.get_barrier_semaphore()
    peers = [member(lax.rem(p + k, POOL)) for k in range(1, POOL)]
    peers += [device_at(lax.rem(x + o, NX), y, z, c) for o in range(1, NX)]
    peers += list(to_z)
    for peer in peers:
        pl.semaphore_signal(barrier, inc=1, device_id=peer, device_id_type=MESH)

    pairs = (
        (routes_hbm, routes_ref),
        (combine_hbm, combine_ref),
        (tok_hbm, tok_v),
        (gu_codes_hbm, gu_codes_ref),
        (gu_scales_hbm, gu_scales_ref),
        (d_codes_hbm, d_codes_ref),
        (d_scales_hbm, d_scales_ref),
        (cot_hbm, cot_v),
    )
    loads = [
        pltpu.make_async_copy(src, dst, load_sem.at[4 + i])
        for i, (src, dst) in enumerate(pairs)
    ]
    for one in loads:
        one.start()

    loads[0].wait()
    loads[1].wait()
    masks, weights = [], []
    for e in range(NX):
        chosen = routes_ref[...] == e
        masks.append(jnp.max(chosen.astype(F32), axis=0, keepdims=True))
        weights.append(
            jnp.sum(jnp.where(chosen, combine_ref[...], 0.0), axis=0, keepdims=True)
        )
    mask = jnp.concatenate(masks + [jnp.zeros((4, TOK), F32)], axis=0)
    before = (iota((TOK, TOK), 0) <= iota((TOK, TOK), 1)).astype(F32).astype(BF16)
    count = dot(mask.astype(BF16), before)
    place = jnp.where(mask > 0.0, count - 1.0, -1.0).astype(jnp.int32)
    wide = (MAIN, TOK)
    place = jnp.concatenate(
        [jnp.broadcast_to(place[e : e + 1], wide) for e in range(NX)], axis=0
    )
    weight = jnp.concatenate(
        [jnp.broadcast_to(weights[e], wide) for e in range(NX)], axis=0
    )
    slot = lax.rem(iota((NX * MAIN, TOK), 0), MAIN)
    is_main = place == slot
    is_tail = place == MAIN + lax.rem(slot, TAIL)
    main_weight = jnp.sum(jnp.where(is_main, weight, 0.0), axis=1, keepdims=True)
    tail_weight = jnp.sum(jnp.where(is_tail, weight, 0.0), axis=1, keepdims=True)
    pick_main = is_main.astype(F32).astype(BF16)
    picks = []
    for k in range(SEG):
        pick_tail = (is_tail & (slot // TAIL == k)).astype(F32).astype(BF16)
        picks.append(jnp.concatenate([pick_main, pick_tail], axis=0))

    def piece(origin, first=0, count=PIECE):
        row = pl.multiple_of((origin // SEG) * PIECE + first, 16)
        column = pl.multiple_of(lax.rem(origin, SEG) * QUART, QUART)
        return wfull.at[pl.ds(row, count), pl.ds(column, QUART)]

    def part(index):
        row = pl.multiple_of(zh * PIECE, 16)
        column = pl.multiple_of(zl * QUART + index * FEAT, FEAT)
        return wfull.at[pl.ds(row, PIECE), pl.ds(column, FEAT)]

    def for_expert(which, e):
        return sbuf.at[which, pl.ds(pl.multiple_of(e * MAIN, MAIN), MAIN), :]

    def rows_of(group, at_y, at_c):
        row = group * PMAIN + (at_y * NC + at_c) * MAIN
        return pl.ds(pl.multiple_of(row, MAIN), MAIN)

    def block(group, at_y, at_c):
        return xbuf.at[:, rows_of(group, at_y, at_c), :]

    def one_block(which, group, at_y, at_c):
        return xbuf.at[which, rows_of(group, at_y, at_c), :]

    def own_part_of(which, group):
        return one_block(which, group, y, c)

    def spread(which, group):
        if group == 0:
            source = for_expert(which, x)
        else:
            source = own_part_of(which, group)
            arrived(source, x_s.at[which, group - 1], x_r.at[which, group - 1])
        for way in range(2):
            send(
                source,
                own_part_of(which, group),
                y_s.at[which, way, group],
                y_r.at[which, way, group],
                to_y[way],
            )
        sems = p_s.at[group, 5 * which], p_r.at[group, 5 * which]
        send(source, own_part_of(which, group), *sems, partner)

    for one in loads[3:7]:
        one.wait()
    lane_block = iota((HID, FEAT), 1) // BLOCK
    for g in range(2):
        rows = pl.ds(g * HID, HID)
        padding = jnp.zeros((FEAT - FEAT // BLOCK, HID), F32)
        turned = jnp.concatenate([gu_scales_ref[g], padding], axis=0).T
        scale = jnp.zeros((HID, FEAT), F32)
        for b in range(FEAT // BLOCK):
            scale = jnp.where(lane_block == b, turned[:, b : b + 1], scale)
        weight = (scale * decode_values(gu_codes_ref[rows, :])).astype(BF16)
        for m in range(POOL):
            wsend[m, g * SUB : (g + 1) * SUB, :] = weight[m * SUB : (m + 1) * SUB, :]
    for m in range(POOL):
        values = decode_values(d_codes_ref[m * SUB : (m + 1) * SUB, :])
        wsend[m, 2 * SUB : 3 * SUB, :] = (d_scales_ref[m : m + 1, :] * values).astype(BF16)

    wide = QUART // NY
    own_rows = []
    for which, (source, load) in enumerate(((tok_v, loads[2]), (cot_v, loads[7]))):
        load.wait()
        for quarter in range(NY):
            folded = jnp.zeros((NX * MAIN, wide), F32)
            for k in range(SEG):
                first = quarter * QUART + k * wide
                both = dot(picks[k], source[:, first : first + wide])
                picked = both[: NX * MAIN]
                folded = folded + both[NX * MAIN :]
                if which == 1:
                    picked = picked * main_weight
                to = k * QUART + quarter * wide
                sbuf[which, :, to : to + wide] = picked.astype(BF16)
            if which == 1:
                folded = folded * tail_weight
            to = D + quarter * wide
            sbuf[which, :, to : to + wide] = folded.astype(BF16)
        if which == 0:
            pl.semaphore_wait(barrier, len(peers))
            own_part = pltpu.make_async_copy(wsend.at[p], part(p), load_sem.at[2])
            own_part.start()
            for k in range(1, POOL):
                to = lax.rem(p + k, POOL)
                send(wsend.at[to], part(p), a_s.at[k - 1], a_r.at[k - 1], member(to))
        for group in range(1, NX):
            e = lax.rem(x + OFFSETS[group], NX)
            send(
                for_expert(which, e),
                own_part_of(which, group),
                x_s.at[which, group - 1],
                x_r.at[which, group - 1],
                device_at(e, y, z, c),
            )
        spread(which, 0)
        own_rows.append(
            pltpu.make_async_copy(
                for_expert(which, x), own_part_of(which, 0), load_sem.at[which]
            )
        )
        own_rows[which].start()

    def relay(group):
        for way in range(2):
            from_y = (y_dn, y_up)[way]
            whole = block(group, from_y, c)
            for which in range(2):
                half = one_block(which, group, from_y, c)
                arrived(half, y_s.at[which, way, group], y_r.at[which, way, group])
            half = one_block(way, group, from_y, c)
            send(half, half, y_s.at[2, way, group], y_r.at[2, way, group], to_y[way])
            send(whole, whole, p_s.at[group, 1 + way], p_r.at[group, 1 + way], partner)

    def relay_far(group):
        for way in range(2):
            half = one_block(way, group, y_far, c)
            arrived(half, y_s.at[2, way, group], y_r.at[2, way, group])
            send(half, half, p_s.at[group, 3 + way], p_r.at[group, 3 + way], partner)

    def all_rows(group):
        for which in range(2):
            half = one_block(which, group, y, oc)
            arrived(half, p_s.at[group, 5 * which], p_r.at[group, 5 * which])
        arrived(block(group, y_dn, oc), p_s.at[group, 1], p_r.at[group, 1])
        arrived(block(group, y_up, oc), p_s.at[group, 2], p_r.at[group, 2])
        for way in range(2):
            half = one_block(way, group, y_far, oc)
            arrived(half, p_s.at[group, 3 + way], p_r.at[group, 3 + way])

    def ways_of(step, half):
        return range(2) if step < STEPS else (half,)

    def weights_on(step, half):
        for way in ways_of(step, half):
            back = NZ - (step - 1) if way == 0 else step - 1
            ref = piece(lax.rem(z + back, NZ), half * HALF, HALF)
            sems = w_s.at[way, step - 1, half], w_r.at[way, step - 1, half]
            send(ref, ref, *sems, to_z[way])

    def weights_in(step, half):
        for way in ways_of(step, half):
            back = NZ - step if way == 0 else step
            ref = piece(lax.rem(z + back, NZ), half * HALF, HALF)
            arrived(ref, w_s.at[way, step - 1, half], w_r.at[way, step - 1, half])
        if step < STEPS:
            weights_on(step + 1, half)

    fold_from = iota((PMAIN, PMAIN), 1)
    fold_to = iota((PMAIN, PMAIN), 0)
    inside = lax.rem(fold_to, PTAIL)
    wanted = (inside // TAIL) * MAIN + (fold_to // PTAIL) * TAIL + lax.rem(inside, TAIL)
    unfold = (fold_from == wanted).astype(F32).astype(BF16)

    def unpack(group):
        all_rows(group)
        for which in range(2):
            folded = xbuf[which, group * PMAIN : (group + 1) * PMAIN, D:PACK]
            tails = dot(unfold, folded).astype(BF16)
            for k in range(SEG):
                xtail[
                    which,
                    group * PTAIL : (group + 1) * PTAIL,
                    k * QUART : (k + 1) * QUART,
                ] = tails[k * PTAIL : (k + 1) * PTAIL, :]

    def gradients(gate, up, back):
        sig = jax.nn.sigmoid(gate)
        to_gate = back * up * sig * (1.0 + gate * (1.0 - sig))
        to_up = back * (gate * sig)
        return to_gate.T.astype(BF16), to_up.T.astype(BF16)

    depth = 2048

    def forward(group):
        rows = pl.ds(group * PMAIN, PMAIN)
        tails = pl.ds(group * PTAIL, PTAIL)

        def one(step, total):
            columns = pl.ds(pl.multiple_of(step * depth, depth), depth)

            def side(kind):
                return [
                    wfull[q * PIECE + kind * SUB : q * PIECE + (kind + 1) * SUB, columns]
                    for q in range(SEG)
                ]

            gate_up = jnp.concatenate(side(0) + side(1), axis=0)
            down = jnp.concatenate(side(2), axis=0)
            tokens = jnp.concatenate([xbuf[0, rows, columns], xtail[0, tails, columns]], 0)
            scaled = jnp.concatenate([xbuf[1, rows, columns], xtail[1, tails, columns]], 0)
            return total[0] + nt_dot(tokens, gate_up), total[1] + nt_dot(scaled, down)

        count = PMAIN + PTAIL
        start = (jnp.zeros((count, 2 * WIDTH), F32), jnp.zeros((count, WIDTH), F32))
        front, back = lax.fori_loop(0, D // depth, one, start)
        to_gate, to_up = gradients(
            front[:PMAIN, :WIDTH], front[:PMAIN, WIDTH:], back[:PMAIN]
        )
        g_t[:WIDTH, rows] = to_gate
        g_t[WIDTH:, rows] = to_up
        pre_tail[tails, : 2 * WIDTH] = front[PMAIN:]
        pre_tail[tails, 2 * WIDTH :] = back[PMAIN:]

    own_part.wait()
    for k in range(1, POOL):
        got = part(lax.rem(p + POOL - k, POOL))
        arrived(got, a_s.at[k - 1], a_r.at[k - 1])
    weights_on(1, 0)
    weights_on(1, 1)

    weights_in(1, 0)
    spread(0, 1)
    spread(0, 2)
    weights_in(1, 1)
    relay(0)
    spread(0, 3)
    weights_in(2, 0)
    weights_in(2, 1)
    spread(1, 1)
    spread(1, 2)
    weights_in(3, 0)
    weights_in(3, 1)
    spread(1, 3)
    weights_in(4, 0)
    weights_in(4, 1)
    for one in own_rows:
        one.wait()
    weights_in(5, 0)
    weights_in(5, 1)
    weights_in(6, 0)
    weights_in(6, 1)
    relay(1)
    weights_in(7, 0)
    relay_far(0)
    weights_in(7, 1)
    relay(2)
    weights_in(8, 0)
    weights_in(8, 1)
    relay(3)
    unpack(0)
    forward(0)
    relay_far(1)
    unpack(1)
    forward(1)
    relay_far(2)
    unpack(2)
    forward(2)
    relay_far(3)
    unpack(3)
    forward(3)
    to_gate, to_up = gradients(
        pre_tail[:, :WIDTH], pre_tail[:, WIDTH : 2 * WIDTH], pre_tail[:, 2 * WIDTH :]
    )
    g_t[:WIDTH, ROWS:] = to_gate
    g_t[WIDTH:, ROWS:] = to_up

    def turn_y(turn):
        return lax.rem(y + 1 + turn, NY)

    def columns_of(turn):
        return pl.ds(pl.multiple_of(turn_y(turn) * PART, PART), PART)

    def weight_gradient(ahead, turn):
        at = lax.rem(zl + ahead, SEG)
        first = pl.multiple_of(at * QUART + turn_y(turn) * PART, PART)
        total = dot(g_t[:, :ROWS], xbuf[0, :, pl.ds(first, PART)])
        total = total + dot(g_t[:, ROWS:], xtail[0, :, pl.ds(first, PART)])
        dw[at, :, columns_of(turn)] = total

    def own_term(dest, kind, turn):
        row = pl.multiple_of(kind * WIDTH + (dest // SEG) * SUB, SUB)
        return dw[lax.rem(dest, SEG), pl.ds(row, SUB), columns_of(turn)]

    def sum_part(ref, step, way, turn):
        if step == 0:
            return ref.at[way, step, turn, way * SUB : (way + 1) * SUB, :]
        return ref.at[way, step, turn]

    def sum_in(step, way, turn):
        ref = sum_part(rs_in, step, way, turn)
        arrived(ref, r_s.at[way, step, turn], r_r.at[way, step, turn])

    def came(step, way, turn, kind):
        return rs_in[way, step, turn, kind * SUB : (kind + 1) * SUB, :].astype(F32)

    def sum_on(step, turn):
        for way in range(2):
            if step > 0:
                sum_in(step - 1, way, turn)
            ahead = STEPS - step if way == 0 else NZ - STEPS + step
            for kind in range(2):
                if step == 0 and kind != way:
                    continue
                total = own_term(lax.rem(z + ahead, NZ), kind, turn)
                if step > 1 or (step == 1 and kind == way):
                    total = total + came(step - 1, way, turn, kind)
                rows = slice(kind * SUB, (kind + 1) * SUB)
                rs_out[way, step, turn, rows, :] = total.astype(BF16)
            send(
                sum_part(rs_out, step, way, turn),
                sum_part(rs_in, step, way, turn),
                r_s.at[way, step, turn],
                r_r.at[way, step, turn],
                to_z[way],
            )

    own_sum = pltpu.make_async_copy(fin_out.at[p], fin_in.at[p], load_sem.at[3])

    def sum_out(turn):
        for way in range(2):
            sum_in(STEPS - 1, way, turn)
        to_y_here = turn_y(turn)
        for kind in range(2):
            total = own_term(z, kind, turn)
            for way in range(2):
                total = total + came(STEPS - 1, way, turn, kind)
            total = total.astype(BF16)
            for core in range(NC):
                fin_out[to_y_here * NC + core, kind * SUB : (kind + 1) * SUB, :] = total[
                    :, core * FEAT : (core + 1) * FEAT
                ]
        for other in range(NC):
            if turn == NY - 1 and other == 0:
                own_sum.start()
                continue
            to = to_y_here * NC + lax.rem(c + other, NC)
            sems = f_s.at[turn, other], f_r.at[turn, other]
            send(fin_out.at[to], fin_in.at[p], *sems, member(to))

    for turn in range(NY):
        weight_gradient(0, turn)
        sum_on(0, turn)
    for turn in range(NY):
        weight_gradient(1, turn)
        weight_gradient(3, turn)
        sum_on(1, turn)
    for turn in range(NY):
        weight_gradient(2, turn)
        sum_on(2, turn)
    for step in range(3, STEPS):
        for turn in range(NY):
            sum_on(step, turn)
    for turn in range(NY):
        sum_out(turn)
    for one in started:
        one.wait_send()
    own_sum.wait()
    for turn in range(NY):
        for other in range(NC):
            if turn == NY - 1 and other == 0:
                continue
            origin = lax.rem(y + NY - 1 - turn, NY) * NC + lax.rem(c + other, NC)
            arrived(fin_in.at[origin], f_s.at[turn, other], f_r.at[turn, other])

    to_block = (iota((8, FEAT), 1) // BLOCK == iota((8, FEAT), 0)).astype(F32)
    for kind in range(2):
        summed = jnp.concatenate(
            [fin_in[m, kind * SUB : (kind + 1) * SUB, :] for m in range(POOL)], axis=0
        ).astype(F32)
        codes = gu_codes_ref[kind * HID : (kind + 1) * HID, :]
        grad_ref[kind * HID : (kind + 1) * HID, :] = jnp.where(codes % 8 != 7, summed, 0.0)
        blocks = lax.dot_general(
            to_block,
            summed * decode_values(codes),
            (((1,), (1,)), ((), ())),
            precision=lax.Precision.HIGHEST,
            preferred_element_type=F32,
        )
        scale_ref[kind] = LSQ * blocks[: FEAT // BLOCK]


def body(tokens, cotangent, routes, combine, gu_codes, gu_scales, d_codes, d_scales):
    hidden, width = gu_codes.shape[1], gu_codes.shape[2]
    vmem = pl.BlockSpec(memory_space=pltpu.VMEM)
    hbm = pl.BlockSpec(memory_space=pl.ANY)
    dma = pltpu.SemaphoreType.DMA
    grad, scale = pl.pallas_call(
        kernel,
        out_shape=(
            jax.ShapeDtypeStruct((2 * hidden, width), F32),
            jax.ShapeDtypeStruct((2, width // BLOCK, hidden), F32),
        ),
        in_specs=[hbm] * 8,
        out_specs=(vmem, vmem),
        scratch_shapes=[
            pltpu.VMEM((TOK, D), BF16),
            pltpu.VMEM((TOK, D), BF16),
            pltpu.VMEM(routes.shape[::-1], jnp.int32),
            pltpu.VMEM(combine.shape[::-1], F32),
            pltpu.VMEM((2 * hidden, width), jnp.int32),
            pltpu.VMEM((2, width // BLOCK, hidden), F32),
            pltpu.VMEM(d_codes.shape, jnp.int32),
            pltpu.VMEM(d_scales.shape, F32),
            pltpu.VMEM((2, NX * MAIN, PACK), BF16),
            pltpu.VMEM((2, ROWS, PACK), BF16),
            pltpu.VMEM((2, TAILS, D), BF16),
            pltpu.VMEM((POOL, PIECE, FEAT), BF16),
            pltpu.VMEM((SEG * PIECE, D), BF16),
            pltpu.VMEM((TAILS, 3 * WIDTH), F32),
            pltpu.VMEM((2 * WIDTH, ROWS + TAILS), BF16),
            pltpu.VMEM((SEG, 2 * WIDTH, QUART), F32),
            pltpu.VMEM((2, STEPS, NY, 2 * SUB, PART), BF16),
            pltpu.VMEM((2, STEPS, NY, 2 * SUB, PART), BF16),
            pltpu.VMEM((POOL, 2 * SUB, FEAT), BF16),
            pltpu.VMEM((POOL, 2 * SUB, FEAT), BF16),
            dma((12,)),
            dma((2, NX - 1)),
            dma((2, NX - 1)),
            dma((3, 2, NX)),
            dma((3, 2, NX)),
            dma((NX, 6)),
            dma((NX, 6)),
            dma((POOL - 1,)),
            dma((POOL - 1,)),
            dma((2, STEPS, 2)),
            dma((2, STEPS, 2)),
            dma((2, STEPS, NY)),
            dma((2, STEPS, NY)),
            dma((NY, NC)),
            dma((NY, NC)),
        ],
        compiler_params=pltpu.CompilerParams(
            collective_id=0, has_side_effects=True, vmem_limit_bytes=56 << 20
        ),
        cost_estimate=pl.CostEstimate(
            flops=2 * 640 * D * 5 * WIDTH, bytes_accessed=8 << 20, transcendentals=0
        ),
    )(
        tokens,
        cotangent,
        routes.T,
        combine.T,
        gu_codes.reshape(2 * hidden, width),
        gu_scales.swapaxes(1, 2),
        d_codes,
        d_scales,
    )
    return (
        grad.reshape(2, hidden, width),
        scale.swapaxes(1, 2),
    )


def solution(mesh):
    rows = P(("dp", "tensor"), None)
    return jax.shard_map(
        body,
        mesh=mesh,
        in_specs=(
            rows,
            rows,
            rows,
            rows,
            P(None, "tensor", "dp"),
            P(None, "tensor", "dp"),
            P("tensor", "dp"),
            P("tensor", "dp"),
        ),
        out_specs=(P(None, "tensor", "dp"), P(None, "tensor", "dp")),
        check_vma=False,
    )
```

time: 130 us -> 108 us (0.83)
  Pallas kernels: 124 us -> 105 us
  local copies, waits for them, and re-layouts: 4.88 us -> 2.97 us
    pallas_call x1, Pallas kernels: 124 us -> 105 us  [body(): pl.pallas_call(kernel, out_shape=(jax.ShapeDtypeStruct((2 * hidden, width...]
    unnamed x3 -> x2, local copies, waits for them, and re-layouts: 4.88 us -> 2.97 us
where the time goes in v3:
time: 108 us
  Pallas kernels  105 us (97%)
  local copies, waits for them, and re-layouts  2.97 us (3%)
    pallas_call x1, Pallas kernels, body(): pl.pallas_call(kernel, out_shape=(jax.ShapeDtypeStruct((2 * hidden, width...  105 us
    unnamed x2, local copies, waits for them, and re-layouts  2.97 us

profile of v3, /device:TPU:1, one launch (start us, length us, event | category | flops | bytes accessed | tf_op | source)
XLA Modules:
  0.0 108.1 jit_solution(2853171765956123282)
XLA Ops:
  0.6 104.5 %shard_map.95 = (f32[512,128]{1,0:T(8,128)}, f32[2,4,256]{2,1,0:T(4,128)}) custom-call(bf16[256,4096]{1,0:T(8,128)(2,1)} %tok_hbm.1, bf16[256,4096]{1,0:T(8,128)(2,1)} %cot_hbm.1, s32[8,256]{1,0:T(8,128)} %bitcast.9, f32[8,256]{1,0:T(8,128)} %bitcast.10, s32[512,128]{1,0:T(8,128)} %bitcast.8, f32[2,4,256]{2,1,0:T(4,128)} %bitcast.11, ...), custom_call_target="tpu_custom_call" | custom-call | flops 3355443200 | bytes 8388608 | tf_op jit(solution)/shard_map/pallas_call | solution.py:580
  105.1 1.7 %copy.12 = f32[2,256,128]{2,1,0:T(8,128)} copy(f32[2,256,128]{2,1,0:T(8,128)} %bitcast.6) | data formatting | bytes 524288
  106.8 1.3 %copy.13 = f32[2,256,4]{1,2,0:T(4,128)} copy(f32[2,256,4]{1,2,0:T(4,128)} %bitcast.7) | data formatting | bytes 16384

commit v4 on v3

--- a/solution.py
+++ b/solution.py
@@ -70,8 +70,7 @@
     gu_scales_hbm,
     d_codes_hbm,
     d_scales_hbm,
-    grad_ref,
-    scale_ref,
+    fin_in,
     tok_v,
     cot_v,
     routes_ref,
@@ -85,13 +84,13 @@
     xtail,
     wsend,
     wfull,
+    pre,
     pre_tail,
     g_t,
     dw,
     rs_out,
     rs_in,
     fin_out,
-    fin_in,
     load_sem,
     x_s,
     x_r,
@@ -120,6 +119,10 @@
     z_up, z_dn = lax.rem(z + 1, NZ), lax.rem(z + NZ - 1, NZ)
     to_y = (device_at(x, y_up, z, c), device_at(x, y_dn, z, c))
     to_z = (device_at(x, y, z_up, c), device_at(x, y, z_dn, c))
+    over_z = (
+        device_at(x, y, lax.rem(z + 2, NZ), c),
+        device_at(x, y, lax.rem(z + NZ - 2, NZ), c),
+    )
     partner = device_at(x, y, z, oc)
 
     def member(index):
@@ -148,7 +151,7 @@
     barrier = pltpu.get_barrier_semaphore()
     peers = [member(lax.rem(p + k, POOL)) for k in range(1, POOL)]
     peers += [device_at(lax.rem(x + o, NX), y, z, c) for o in range(1, NX)]
-    peers += list(to_z)
+    peers += list(to_z) + list(over_z)
     for peer in peers:
         pl.semaphore_signal(barrier, inc=1, device_id=peer, device_id_type=MESH)
 
@@ -372,14 +375,18 @@
         to_up = back * (gate * sig)
         return to_gate.T.astype(BF16), to_up.T.astype(BF16)
 
-    depth = 2048
-
-    def forward(group):
+    def forward(group, quarters, first, last):
         rows = pl.ds(group * PMAIN, PMAIN)
         tails = pl.ds(group * PTAIL, PTAIL)
-
-        def one(step, total):
-            columns = pl.ds(pl.multiple_of(step * depth, depth), depth)
+        count = PMAIN + PTAIL
+        if first:
+            front = jnp.zeros((count, 2 * WIDTH), F32)
+            back = jnp.zeros((count, WIDTH), F32)
+        else:
+            front, back = pre[group, :, : 2 * WIDTH], pre[group, :, 2 * WIDTH :]
+        for quarter in quarters:
+            at = pl.multiple_of(lax.rem(zl + quarter, SEG) * QUART, QUART)
+            columns = pl.ds(at, QUART)
 
             def side(kind):
                 return [
@@ -391,11 +398,12 @@
             down = jnp.concatenate(side(2), axis=0)
             tokens = jnp.concatenate([xbuf[0, rows, columns], xtail[0, tails, columns]], 0)
             scaled = jnp.concatenate([xbuf[1, rows, columns], xtail[1, tails, columns]], 0)
-            return total[0] + nt_dot(tokens, gate_up), total[1] + nt_dot(scaled, down)
-
-        count = PMAIN + PTAIL
-        start = (jnp.zeros((count, 2 * WIDTH), F32), jnp.zeros((count, WIDTH), F32))
-        front, back = lax.fori_loop(0, D // depth, one, start)
+            front = front + nt_dot(tokens, gate_up)
+            back = back + nt_dot(scaled, down)
+        if not last:
+            pre[group, :, : 2 * WIDTH] = front
+            pre[group, :, 2 * WIDTH :] = back
+            return
         to_gate, to_up = gradients(
             front[:PMAIN, :WIDTH], front[:PMAIN, WIDTH:], back[:PMAIN]
         )
@@ -430,27 +438,31 @@
         one.wait()
     weights_in(5, 0)
     weights_in(5, 1)
+    relay(1)
     weights_in(6, 0)
+    relay_far(0)
     weights_in(6, 1)
-    relay(1)
+    relay(2)
+    unpack(0)
+    forward(0, (2,), True, False)
     weights_in(7, 0)
-    relay_far(0)
     weights_in(7, 1)
-    relay(2)
+    forward(0, (1, 3), False, False)
+    relay(3)
+    relay_far(1)
+    unpack(1)
+    forward(1, (2, 1, 3), True, False)
+    relay_far(2)
+    unpack(2)
+    forward(2, (2, 1, 3), True, False)
     weights_in(8, 0)
     weights_in(8, 1)
-    relay(3)
-    unpack(0)
-    forward(0)
-    relay_far(1)
-    unpack(1)
-    forward(1)
-    relay_far(2)
-    unpack(2)
-    forward(2)
+    forward(0, (0,), False, True)
+    forward(1, (0,), False, True)
+    forward(2, (0,), False, True)
     relay_far(3)
     unpack(3)
-    forward(3)
+    forward(3, (0, 1, 2, 3), True, True)
     to_gate, to_up = gradients(
         pre_tail[:, :WIDTH], pre_tail[:, WIDTH : 2 * WIDTH], pre_tail[:, 2 * WIDTH :]
     )
@@ -488,15 +500,19 @@
 
     def sum_on(step, turn):
         for way in range(2):
-            if step > 0:
+            if step > 1:
                 sum_in(step - 1, way, turn)
+            if step == 2:
+                sum_in(0, way, turn)
             ahead = STEPS - step if way == 0 else NZ - STEPS + step
             for kind in range(2):
                 if step == 0 and kind != way:
                     continue
                 total = own_term(lax.rem(z + ahead, NZ), kind, turn)
-                if step > 1 or (step == 1 and kind == way):
+                if step > 1:
                     total = total + came(step - 1, way, turn, kind)
+                if step == 2 and kind == way:
+                    total = total + came(0, way, turn, kind)
                 rows = slice(kind * SUB, (kind + 1) * SUB)
                 rs_out[way, step, turn, rows, :] = total.astype(BF16)
             send(
@@ -504,7 +520,7 @@
                 sum_part(rs_in, step, way, turn),
                 r_s.at[way, step, turn],
                 r_r.at[way, step, turn],
-                to_z[way],
+                (over_z if step == 0 else to_z)[way],
             )
 
     own_sum = pltpu.make_async_copy(fin_out.at[p], fin_in.at[p], load_sem.at[3])
@@ -533,7 +549,6 @@
     for turn in range(NY):
         weight_gradient(0, turn)
         sum_on(0, turn)
-    for turn in range(NY):
         weight_gradient(1, turn)
         weight_gradient(3, turn)
         sum_on(1, turn)
@@ -555,12 +570,14 @@
             origin = lax.rem(y + NY - 1 - turn, NY) * NC + lax.rem(c + other, NC)
             arrived(fin_in.at[origin], f_s.at[turn, other], f_r.at[turn, other])
 
+
+def finish(sums_ref, codes_ref, grad_ref, scale_ref):
     to_block = (iota((8, FEAT), 1) // BLOCK == iota((8, FEAT), 0)).astype(F32)
     for kind in range(2):
         summed = jnp.concatenate(
-            [fin_in[m, kind * SUB : (kind + 1) * SUB, :] for m in range(POOL)], axis=0
+            [sums_ref[m, kind * SUB : (kind + 1) * SUB, :] for m in range(POOL)], axis=0
         ).astype(F32)
-        codes = gu_codes_ref[kind * HID : (kind + 1) * HID, :]
+        codes = codes_ref[kind * HID : (kind + 1) * HID, :]
         grad_ref[kind * HID : (kind + 1) * HID, :] = jnp.where(codes % 8 != 7, summed, 0.0)
         blocks = lax.dot_general(
             to_block,
@@ -571,20 +588,17 @@
         )
         scale_ref[kind] = LSQ * blocks[: FEAT // BLOCK]
 
-
 def body(tokens, cotangent, routes, combine, gu_codes, gu_scales, d_codes, d_scales):
     hidden, width = gu_codes.shape[1], gu_codes.shape[2]
     vmem = pl.BlockSpec(memory_space=pltpu.VMEM)
     hbm = pl.BlockSpec(memory_space=pl.ANY)
     dma = pltpu.SemaphoreType.DMA
-    grad, scale = pl.pallas_call(
+    codes = gu_codes.reshape(2 * hidden, width)
+    sums = pl.pallas_call(
         kernel,
-        out_shape=(
-            jax.ShapeDtypeStruct((2 * hidden, width), F32),
-            jax.ShapeDtypeStruct((2, width // BLOCK, hidden), F32),
-        ),
+        out_shape=jax.ShapeDtypeStruct((POOL, 2 * SUB, FEAT), BF16),
         in_specs=[hbm] * 8,
-        out_specs=(vmem, vmem),
+        out_specs=hbm,
         scratch_shapes=[
             pltpu.VMEM((TOK, D), BF16),
             pltpu.VMEM((TOK, D), BF16),
@@ -599,12 +613,12 @@
             pltpu.VMEM((2, TAILS, D), BF16),
             pltpu.VMEM((POOL, PIECE, FEAT), BF16),
             pltpu.VMEM((SEG * PIECE, D), BF16),
+            pltpu.VMEM((NX, PMAIN + PTAIL, 3 * WIDTH), F32),
             pltpu.VMEM((TAILS, 3 * WIDTH), F32),
             pltpu.VMEM((2 * WIDTH, ROWS + TAILS), BF16),
             pltpu.VMEM((SEG, 2 * WIDTH, QUART), F32),
             pltpu.VMEM((2, STEPS, NY, 2 * SUB, PART), BF16),
             pltpu.VMEM((2, STEPS, NY, 2 * SUB, PART), BF16),
-            pltpu.VMEM((POOL, 2 * SUB, FEAT), BF16),
             pltpu.VMEM((POOL, 2 * SUB, FEAT), BF16),
             dma((12,)),
             dma((2, NX - 1)),
@@ -633,11 +647,20 @@
         cotangent,
         routes.T,
         combine.T,
-        gu_codes.reshape(2 * hidden, width),
+        codes,
         gu_scales.swapaxes(1, 2),
         d_codes,
         d_scales,
     )
+    grad, scale = pl.pallas_call(
+        finish,
+        out_shape=(
+            jax.ShapeDtypeStruct((2 * hidden, width), F32),
+            jax.ShapeDtypeStruct((2, width // BLOCK, hidden), F32),
+        ),
+        in_specs=[vmem] * 2,
+        out_specs=(vmem, vmem),
+    )(sums, codes)
     return (
         grad.reshape(2, hidden, width),
         scale.swapaxes(1, 2),

time: 108 us -> 102 us (0.944)
  Pallas kernels: 105 us -> 101 us
  local copies, waits for them, and re-layouts: 2.97 us -> 0 us
    pallas_call x1 -> x2, Pallas kernels: 105 us -> 101 us  [the longest x1 98.8 us: body(): pl.pallas_call(kernel, out_shape=jax.ShapeDtypeStruct((POOL, 2 * SUB, FEA...]
    unnamed x2 -> x0, local copies, waits for them, and re-layouts: 2.97 us -> none
where the time goes in v4:
time: 102 us
  Pallas kernels  101 us (99%)
    pallas_call x1, Pallas kernels, body(): pl.pallas_call(kernel, out_shape=jax.ShapeDtypeStruct((POOL, 2 * SUB, FEA...  98.8 us
    pallas_call x1, Pallas kernels, body(): pl.pallas_call(finish, out_shape=(jax.ShapeDtypeStruct((2 * hidden, width...  2.17 us

profile of v4, /device:TPU:1, one launch (start us, length us, event | category | flops | bytes accessed | tf_op | source)
XLA Modules:
  0.0 101.6 jit_solution(3565988578110315667)
XLA Ops:
  0.6 98.8 %shard_map.95.sums_ref = bf16[8,64,128]{2,1,0:T(8,128)(2,1)} custom-call(bf16[256,4096]{1,0:T(8,128)(2,1)} %tok_hbm.1, bf16[256,4096]{1,0:T(8,128)(2,1)} %cot_hbm.1, s32[8,256]{1,0:T(8,128)} %bitcast.9, f32[8,256]{1,0:T(8,128)} %bitcast.10, s32[512,128]{1,0:T(8,128)} %bitcast.6, f32[2,4,256]{2,1,0:T(4,128)} %bitcast.11, s32[256,128]{1,0:T(8,128)} %d_codes_hbm.1, ...), custom_call_target="tpu_custom_call" | custom-call | flops 3355443200 | bytes 8388608 | tf_op jit(solution)/shard_map/pallas_call | solution.py:597
  99.4 2.2 %shard_map.96 = (f32[512,128]{1,0:T(8,128)}, f32[2,4,256]{2,1,0:T(4,128)}) custom-call(bf16[8,64,128]{2,1,0:T(8,128)(2,1)} %shard_map.95.sums_ref, s32[512,128]{1,0:T(8,128)} %bitcast.7), custom_call_target="tpu_custom_call" | custom-call | tf_op jit(solution)/shard_map/pallas_call | solution.py:655

commit v5 on v4

--- a/solution.py
+++ b/solution.py
@@ -156,13 +156,13 @@
         pl.semaphore_signal(barrier, inc=1, device_id=peer, device_id_type=MESH)
 
     pairs = (
-        (routes_hbm, routes_ref),
-        (combine_hbm, combine_ref),
-        (tok_hbm, tok_v),
         (gu_codes_hbm, gu_codes_ref),
         (gu_scales_hbm, gu_scales_ref),
         (d_codes_hbm, d_codes_ref),
         (d_scales_hbm, d_scales_ref),
+        (routes_hbm, routes_ref),
+        (combine_hbm, combine_ref),
+        (tok_hbm, tok_v),
         (cot_hbm, cot_v),
     )
     loads = [
@@ -171,37 +171,6 @@
     ]
     for one in loads:
         one.start()
-
-    loads[0].wait()
-    loads[1].wait()
-    masks, weights = [], []
-    for e in range(NX):
-        chosen = routes_ref[...] == e
-        masks.append(jnp.max(chosen.astype(F32), axis=0, keepdims=True))
-        weights.append(
-            jnp.sum(jnp.where(chosen, combine_ref[...], 0.0), axis=0, keepdims=True)
-        )
-    mask = jnp.concatenate(masks + [jnp.zeros((4, TOK), F32)], axis=0)
-    before = (iota((TOK, TOK), 0) <= iota((TOK, TOK), 1)).astype(F32).astype(BF16)
-    count = dot(mask.astype(BF16), before)
-    place = jnp.where(mask > 0.0, count - 1.0, -1.0).astype(jnp.int32)
-    wide = (MAIN, TOK)
-    place = jnp.concatenate(
-        [jnp.broadcast_to(place[e : e + 1], wide) for e in range(NX)], axis=0
-    )
-    weight = jnp.concatenate(
-        [jnp.broadcast_to(weights[e], wide) for e in range(NX)], axis=0
-    )
-    slot = lax.rem(iota((NX * MAIN, TOK), 0), MAIN)
-    is_main = place == slot
-    is_tail = place == MAIN + lax.rem(slot, TAIL)
-    main_weight = jnp.sum(jnp.where(is_main, weight, 0.0), axis=1, keepdims=True)
-    tail_weight = jnp.sum(jnp.where(is_tail, weight, 0.0), axis=1, keepdims=True)
-    pick_main = is_main.astype(F32).astype(BF16)
-    picks = []
-    for k in range(SEG):
-        pick_tail = (is_tail & (slot // TAIL == k)).astype(F32).astype(BF16)
-        picks.append(jnp.concatenate([pick_main, pick_tail], axis=0))
 
     def piece(origin, first=0, count=PIECE):
         row = pl.multiple_of((origin // SEG) * PIECE + first, 16)
@@ -246,7 +215,7 @@
         sems = p_s.at[group, 5 * which], p_r.at[group, 5 * which]
         send(source, own_part_of(which, group), *sems, partner)
 
-    for one in loads[3:7]:
+    for one in loads[:4]:
         one.wait()
     lane_block = iota((HID, FEAT), 1) // BLOCK
     for g in range(2):
@@ -263,9 +232,47 @@
         values = decode_values(d_codes_ref[m * SUB : (m + 1) * SUB, :])
         wsend[m, 2 * SUB : 3 * SUB, :] = (d_scales_ref[m : m + 1, :] * values).astype(BF16)
 
+    pl.semaphore_wait(barrier, len(peers))
+    own_part = pltpu.make_async_copy(wsend.at[p], part(p), load_sem.at[2])
+    own_part.start()
+    for k in range(1, POOL):
+        to = lax.rem(p + k, POOL)
+        send(wsend.at[to], part(p), a_s.at[k - 1], a_r.at[k - 1], member(to))
+
+    loads[4].wait()
+    loads[5].wait()
+    masks, weights = [], []
+    for e in range(NX):
+        chosen = routes_ref[...] == e
+        masks.append(jnp.max(chosen.astype(F32), axis=0, keepdims=True))
+        weights.append(
+            jnp.sum(jnp.where(chosen, combine_ref[...], 0.0), axis=0, keepdims=True)
+        )
+    mask = jnp.concatenate(masks + [jnp.zeros((4, TOK), F32)], axis=0)
+    before = (iota((TOK, TOK), 0) <= iota((TOK, TOK), 1)).astype(F32).astype(BF16)
+    count = dot(mask.astype(BF16), before)
+    place = jnp.where(mask > 0.0, count - 1.0, -1.0).astype(jnp.int32)
+    wide = (MAIN, TOK)
+    place = jnp.concatenate(
+        [jnp.broadcast_to(place[e : e + 1], wide) for e in range(NX)], axis=0
+    )
+    weight = jnp.concatenate(
+        [jnp.broadcast_to(weights[e], wide) for e in range(NX)], axis=0
+    )
+    slot = lax.rem(iota((NX * MAIN, TOK), 0), MAIN)
+    is_main = place == slot
+    is_tail = place == MAIN + lax.rem(slot, TAIL)
+    main_weight = jnp.sum(jnp.where(is_main, weight, 0.0), axis=1, keepdims=True)
+    tail_weight = jnp.sum(jnp.where(is_tail, weight, 0.0), axis=1, keepdims=True)
+    pick_main = is_main.astype(F32).astype(BF16)
+    picks = []
+    for k in range(SEG):
+        pick_tail = (is_tail & (slot // TAIL == k)).astype(F32).astype(BF16)
+        picks.append(jnp.concatenate([pick_main, pick_tail], axis=0))
+
     wide = QUART // NY
     own_rows = []
-    for which, (source, load) in enumerate(((tok_v, loads[2]), (cot_v, loads[7]))):
+    for which, (source, load) in enumerate(((tok_v, loads[6]), (cot_v, loads[7]))):
         load.wait()
         for quarter in range(NY):
             folded = jnp.zeros((NX * MAIN, wide), F32)
@@ -282,13 +289,6 @@
                 folded = folded * tail_weight
             to = D + quarter * wide
             sbuf[which, :, to : to + wide] = folded.astype(BF16)
-        if which == 0:
-            pl.semaphore_wait(barrier, len(peers))
-            own_part = pltpu.make_async_copy(wsend.at[p], part(p), load_sem.at[2])
-            own_part.start()
-            for k in range(1, POOL):
-                to = lax.rem(p + k, POOL)
-                send(wsend.at[to], part(p), a_s.at[k - 1], a_r.at[k - 1], member(to))
         for group in range(1, NX):
             e = lax.rem(x + OFFSETS[group], NX)
             send(
@@ -310,11 +310,12 @@
         for way in range(2):
             from_y = (y_dn, y_up)[way]
             whole = block(group, from_y, c)
-            for which in range(2):
+            for which in (way, 1 - way):
                 half = one_block(which, group, from_y, c)
                 arrived(half, y_s.at[which, way, group], y_r.at[which, way, group])
-            half = one_block(way, group, from_y, c)
-            send(half, half, y_s.at[2, way, group], y_r.at[2, way, group], to_y[way])
+                if which == way:
+                    sems = y_s.at[2, way, group], y_r.at[2, way, group]
+                    send(half, half, *sems, to_y[way])
             send(whole, whole, p_s.at[group, 1 + way], p_r.at[group, 1 + way], partner)
 
     def relay_far(group):

time: 102 us -> 102 us (level)
  no operation moved by 1% of the time
where the time goes in v5:
time: 102 us
  Pallas kernels  101 us (99%)
    pallas_call x1, Pallas kernels, body(): pl.pallas_call(kernel, out_shape=jax.ShapeDtypeStruct((POOL, 2 * SUB, FEA...  98.9 us
    pallas_call x1, Pallas kernels, body(): pl.pallas_call(finish, out_shape=(jax.ShapeDtypeStruct((2 * hidden, width...  2.17 us

profile of v5, /device:TPU:1, one launch (start us, length us, event | category | flops | bytes accessed | tf_op | source)
XLA Modules:
  0.0 101.7 jit_solution(17146258236175339458)
XLA Ops:
  0.6 98.9 %shard_map.95.sums_ref = bf16[8,64,128]{2,1,0:T(8,128)(2,1)} custom-call(bf16[256,4096]{1,0:T(8,128)(2,1)} %tok_hbm.1, bf16[256,4096]{1,0:T(8,128)(2,1)} %cot_hbm.1, s32[8,256]{1,0:T(8,128)} %bitcast.9, f32[8,256]{1,0:T(8,128)} %bitcast.10, s32[512,128]{1,0:T(8,128)} %bitcast.6, f32[2,4,256]{2,1,0:T(4,128)} %bitcast.11, s32[256,128]{1,0:T(8,128)} %d_codes_hbm.1, ...), custom_call_target="tpu_custom_call" | custom-call | flops 3355443200 | bytes 8388608 | tf_op jit(solution)/shard_map/pallas_call | solution.py:598
  99.5 2.2 %shard_map.96 = (f32[512,128]{1,0:T(8,128)}, f32[2,4,256]{2,1,0:T(4,128)}) custom-call(bf16[8,64,128]{2,1,0:T(8,128)(2,1)} %shard_map.95.sums_ref, s32[512,128]{1,0:T(8,128)} %bitcast.7), custom_call_target="tpu_custom_call" | custom-call | tf_op jit(solution)/shard_map/pallas_call | solution.py:656
